TPU v7x, 512 devices: a whole 4x4x16 slice. The times are simulated.
512 devices in a mesh: inst: 64 (over z, y), head: 8 (over x, core).
Axes of the slice: x: 4, y: 4, z: 16, core: 2. Of those that a mesh axis runs over, the one named last changes fastest.
Arguments:
- prefill_codes: bfloat16 [2048, 64, 576], P('inst', 'head'), may hold values from -4 to 4
- prefill_scales: bfloat16 [2048, 64, 4], P('inst', 'head'), may hold values from 0.25 to 1
- page_lists: int32 [2048, 1], P('inst'), may hold values from 0 to 31, as said below
- req_lengths: int32 [2048], P('inst'), may hold values from 1 to 64
- destinations: int32 [2048], P('inst'), may hold values from 0 to 63, as said below
- pool_codes: bfloat16 [1024, 64, 576], P('inst'), may hold values from -4 to 4
- pool_scales: bfloat16 [1024, 64, 4], P('inst'), may hold values from 0.25 to 1
- res_tables: int32 [4096, 8], P('inst'), may hold values from 0 to 15, as said below
- res_lengths: int32 [4096], P('inst'), may hold values from 1 to 512
- queries: bfloat16 [2, 4096, 64, 576], P(None, 'inst', 'head'), may hold values from -48 to 48
- new_latents: bfloat16 [2, 4096, 576], P(None, 'inst'), may hold values from -6 to 6
- value_projection: bfloat16 [64, 512, 128], P('head'), may hold values from -0.75 to 0.75
Outputs:
- attn_out: bfloat16 [2, 4096, 8192], P(None, 'inst', 'head')
Inputs may be any that keep to these rules, and one draw needn't show every extreme that they name: `page_lists`: the 32 requests of one owner list disjoint pages of its own pool, every page once. `destinations`: the 32 requests of one owner go to distinct decode groups; in every draw some group receives a request from every owner. `res_tables`: each row lists 8 distinct pages of its group's resident pages; different rows may list the same pages.
All inputs are finite; a program needn't handle non-finite values.
Results may differ from a plain program's by a relative error of at most 0.0068.
Values may be sent and summed in bfloat16 or wider, within the bound.
A program may use at most 192 MiB of HBM per device.

v0:
```python
import math

import jax
import jax.numpy as jnp
from jax import lax
from jax.sharding import PartitionSpec as P

LATENT_WIDTH = 512
TILE = 128


softmax_scale = (0.1 * math.log(40.0) + 1.0) ** 2 / math.sqrt(192.0)
block_rows = 64


def dequantize(decoded_values, tile_scales):
    spread_rows = jnp.repeat(tile_scales.astype(jnp.float32), TILE, axis=-1)
    latent_state = decoded_values[..., :LATENT_WIDTH].astype(jnp.float32) * spread_rows
    rotary_part = decoded_values[..., LATENT_WIDTH:].astype(jnp.float32)
    return jnp.concatenate([latent_state, rotary_part], axis=-1).astype(jnp.bfloat16)


def to_blocks(array, axis):
    shape = array.shape
    blocks = shape[axis] // block_rows
    split = array.reshape(shape[:axis] + (blocks, block_rows) + shape[axis + 1 :])
    return jnp.moveaxis(split, axis, 0)


def shards(
    prefill_codes,
    prefill_scales,
    page_lists,
    req_lengths,
    destinations,
    pool_codes,
    pool_scales,
    res_tables,
    res_lengths,
    queries,
    new_latents,
    value_projection,
):
    group_count = lax.axis_size("inst")
    request_count = destinations.shape[0]
    row_count = res_tables.shape[0]
    page_size = pool_codes.shape[1]
    pool_pages = pool_codes.shape[0]
    table_width = res_tables.shape[1]
    width = pool_codes.shape[2]
    group_ids = jnp.arange(group_count, dtype=jnp.int32)
    matches = destinations[None, :] == group_ids[:, None]
    present = jnp.any(matches, axis=1)
    chosen = jnp.sum(
        matches.astype(jnp.int32) * jnp.arange(request_count, dtype=jnp.int32)[None, :], axis=1
    )
    slot_pages = page_lists[chosen]
    slot_lengths = jnp.where(present, req_lengths[chosen], 0)
    pool_keys = dequantize(pool_codes, pool_scales)
    flattened_pool = pool_keys.reshape(pool_pages * page_size, width)
    full_codes, full_scales = (
        lax.all_gather(prefill_codes, "head", axis=1, tiled=True),
        lax.all_gather(prefill_scales, "head", axis=1, tiled=True),
    )
    recv_codes, recv_scales, recv_lengths = (
        lax.all_to_all(full_codes[slot_pages], "inst", split_axis=0, concat_axis=0, tiled=True),
        lax.all_to_all(full_scales[slot_pages], "inst", split_axis=0, concat_axis=0, tiled=True),
        lax.all_to_all(slot_lengths, "inst", split_axis=0, concat_axis=0, tiled=True),
    )
    present_src = (recv_lengths > 0).astype(jnp.int32)
    slot_rank = jnp.cumsum(present_src) - 1
    arrivals = jnp.sum(present_src)
    row_ids = jnp.arange(row_count, dtype=jnp.int32)
    picked = (present_src[None, :] == 1) & (slot_rank[None, :] == row_ids[:, None])
    anchor = jnp.sum(picked.astype(jnp.int32) * group_ids[None, :], axis=1)
    arrived = row_ids < arrivals
    arr_len = jnp.where(arrived, recv_lengths[anchor], 0)
    arr_keys = dequantize(recv_codes[anchor], recv_scales[anchor]).reshape(row_count, -1, width)
    arr_mask = jnp.arange(arr_keys.shape[1], dtype=jnp.int32)[None, :] < arr_len[:, None]
    table_hit = res_tables[:, :, None] == jnp.arange(pool_pages, dtype=jnp.int32)[None, None, :]
    listed = jnp.any(table_hit, axis=1)
    start_pos = jnp.sum(
        table_hit.astype(jnp.int32)
        * (jnp.arange(table_width, dtype=jnp.int32) * page_size)[None, :, None],
        axis=1,
    )
    token_pos = start_pos[:, :, None] + jnp.arange(page_size, dtype=jnp.int32)[None, None, :]
    res_valid = (listed[:, :, None] & (token_pos < res_lengths[:, None, None])).reshape(
        row_count, pool_pages * page_size
    )
    res_extra = (res_valid & jnp.logical_not(arrived)[:, None],)

    def run_block(parts):
        query_pair, new_pair, block_arriving, block_arr_mask, extra = parts
        res_mask = extra[0]
        score_form = "rhc,kc->rhk"
        mix_form = "rhk,kc->rhc"
        resident_latent = flattened_pool[..., :LATENT_WIDTH]
        arriving_latent = block_arriving[..., :LATENT_WIDTH]
        outputs = []
        for step_index in range(2):
            step_query = query_pair[step_index]
            fresh_keys = jnp.moveaxis(new_pair[: step_index + 1], 0, 1)
            res_scores = (
                jnp.einsum(
                    score_form, step_query, flattened_pool, preferred_element_type=jnp.float32
                )
                * softmax_scale
            )
            arr_scores = (
                jnp.einsum(
                    "rhc,rkc->rhk", step_query, block_arriving, preferred_element_type=jnp.float32
                )
                * softmax_scale
            )
            new_scores = (
                jnp.einsum(
                    "rhc,rjc->rhj", step_query, fresh_keys, preferred_element_type=jnp.float32
                )
                * softmax_scale
            )
            res_scores = jnp.where(res_mask[:, None, :], res_scores, -jnp.inf)
            arr_scores = jnp.where(block_arr_mask[:, None, :], arr_scores, -jnp.inf)
            highest = jnp.maximum(
                jnp.maximum(
                    jnp.max(res_scores, axis=-1, keepdims=True),
                    jnp.max(arr_scores, axis=-1, keepdims=True),
                ),
                jnp.max(new_scores, axis=-1, keepdims=True),
            )
            res_exp = jnp.exp(res_scores - highest)
            arr_exp = jnp.exp(arr_scores - highest)
            new_exp = jnp.exp(new_scores - highest)
            denominator = (
                jnp.sum(res_exp, axis=-1, keepdims=True)
                + jnp.sum(arr_exp, axis=-1, keepdims=True)
                + jnp.sum(new_exp, axis=-1, keepdims=True)
            )
            res_weights = (res_exp / denominator).astype(jnp.bfloat16)
            arr_weights = (arr_exp / denominator).astype(jnp.bfloat16)
            new_weights = (new_exp / denominator).astype(jnp.bfloat16)
            latent_state = jnp.einsum(
                mix_form, res_weights, resident_latent, preferred_element_type=jnp.float32
            )
            latent_state = latent_state + jnp.einsum(
                "luy,lyb->lub", arr_weights, arriving_latent, preferred_element_type=jnp.float32
            )
            latent_state = latent_state + jnp.einsum(
                "rhj,rjc->rhc",
                new_weights,
                fresh_keys[..., :LATENT_WIDTH],
                preferred_element_type=jnp.float32,
            )
            latent_state = latent_state.astype(jnp.bfloat16)
            mixed_out = jnp.einsum(
                "rhc,hcv->rhv", latent_state, value_projection, preferred_element_type=jnp.float32
            ).astype(jnp.bfloat16)
            outputs.append(mixed_out.reshape(mixed_out.shape[0], -1))
        return jnp.stack(outputs)

    block_extra = tuple((to_blocks(item, 0) for item in res_extra))
    inputs = (
        to_blocks(queries, 1),
        to_blocks(new_latents, 1),
        to_blocks(arr_keys, 0),
        to_blocks(arr_mask, 0),
        block_extra,
    )
    stacked = lax.map(run_block, inputs)
    stacked = jnp.moveaxis(stacked, 0, 1)
    return stacked.reshape(2, row_count, stacked.shape[-1])


def solution(mesh):
    return jax.shard_map(
        shards,
        mesh=mesh,
        in_specs=(
            P("inst", "head", None),
            P("inst", "head", None),
            P("inst", None),
            P("inst"),
            P("inst"),
            P("inst", None, None),
            P("inst", None, None),
            P("inst", None),
            P("inst"),
            P(None, "inst", "head", None),
            P(None, "inst", None),
            P("head", None, None),
        ),
        out_specs=P(None, "inst", "head"),
        check_vma=False,
    )
```

profile of v0, /device:TPU:2, one launch (start us, length us, event | category | flops | bytes accessed | tf_op | source)
XLA Modules:
  0.0 364.0 jit_solution(15928094942598991611)
XLA Ops:
  7.3 0.7 select_reduce_fusion.2
  8.0 1.4 gather_fusion
  9.5 0.8 fusion.55
  10.9 18.7 %all-to-all-start = ((s32[64,1,1]{2,1,0:T(1,128)}), s32[64,1,1]{2,1,0:T(1,128)S(1)}, u32[]{:S(2)}, u32[]{:S(2)}) async-start(s32[64,1,1]{2,1,0:T(1,128)} %copy.173), calls=%async_computation | async-start | bytes 65536 | tf_op jit(solution)/shard_map/all_to_all | solution.py:68
  29.7 1.4 gather_fusion.2
  31.1 13.0 %all_gather.7 = bf16[32,64,4]{0,2,1:T(4,128)(2,1)S(1)} all-gather(bf16[32,8,4]{0,2,1:T(4,128)(2,1)} %param.13), channel_id=1, replica_groups=mesh['inst'=64,'head'=8] {'head'}, dimensions={1}, use_global_device_ids=true | all-gather | bytes 18432 | tf_op jit(solution)/shard_map/all_gather | solution.py:63
  45.7 15.1 %all-to-all-start.2 = ((bf16[64,2,128]{2,1,0:T(2,128)(2,1)}), bf16[64,2,128]{2,1,0:T(2,128)(2,1)S(1)}, u32[]{:S(2)}, u32[]{:S(2)}) async-start(bf16[64,2,128]{2,1,0:T(2,128)(2,1)} %reshape.343), calls=%async_computation.2 | async-start | bytes 65536 | tf_op jit(solution)/shard_map/all_to_all | solution.py:67
  60.8 5.2 %gather_fusion.3 = bf16[64,64,576]{2,1,0:T(8,128)(2,1)} fusion(bf16[32,64,576]{2,1,0:T(8,128)(2,1)} %all-gather.2.cloned.1.call-done, s32[1024]{0:T(1024)S(1)} %pad_clamp_fusion), kind=kCustom, calls=%fused_computation.3 | custom fusion | bytes 9437440 | tf_op jit(solution)/shard_map/gather | solution.py:66
  66.0 9.3 %all-to-all-done.2 = bf16[64,2,128]{2,1,0:T(2,128)(2,1)S(1)} async-done(((bf16[64,2,128]{2,1,0:T(2,128)(2,1)}), bf16[64,2,128]{2,1,0:T(2,128)(2,1)S(1)}, u32[]{:S(2)}, u32[]{:S(2)}) %all-to-all-start.2) | async-done | bytes 32800 | tf_op jit(solution)/shard_map/all_to_all | solution.py:67
  75.4 6.3 %all-to-all-start.1 = ((bf16[64,1,64,576]{3,2,1,0:T(8,128)(2,1)}), bf16[64,1,64,576]{3,2,1,0:T(8,128)(2,1)}, u32[]{:S(2)}, u32[]{:S(2)}) async-start(bf16[64,1,64,576]{3,2,1,0:T(8,128)(2,1)} %bitcast.118), calls=%async_computation.1 | async-start | bytes 10485760 | tf_op jit(solution)/shard_map/all_to_all | solution.py:66
  82.1 0.9 add.113
  83.3 0.8 and.28
  84.8 1.0 copy.174
  85.8 2.2 broadcast_in_dim.110
  88.0 1.9 reshape.264
  89.9 1.7 slice.39
  91.5 2.2 multiply_convert_fusion.1
  93.8 1.3 copy.176
  95.1 1.7 copy.208
  96.9 1.7 copy.240
  98.6 0.9 slice_bitcast_fusion.1
  99.5 1.1 fusion.32
  100.6 1.4 copy.207
  102.0 2.1 fusion.72
  105.4 0.9 fusion.71
  106.7 1.2 reduce
  108.2 0.8 gather_fusion.1
  111.0 0.8 fusion.37
  111.8 3.9 %fusion.75 = (f32[64,8]{0,1:T(8,128)S(1)}, f32[64,8,1024]{2,0,1:T(8,128)}) fusion(bf16[1,64,8,576]{3,2,1,0:T(8,128)(2,1)} %get-tuple-element.23, bf16[1024,64]{0,1:T(8,128)(2,1)} %copy.208, bf16[1024,512]{0,1:T(8,128)(2,1)} %copy.176, pred[64,1024]{1,0:T(8,128)(4,1)S(1)} %fusion.37), kind=kOutput, calls=%fused_computation.136 | convolution fusion | flops 607911424 | bytes 3934208 | tf_op jit(solution)/shard_map/while/body/eval_jaxpr/rhc,kc->rhk/dot_general | solution.py:105
  115.7 2.9 fusion.73
  120.1 7.1 %broadcast_in_dim.113 = f32[64,64,4,128]{3,2,1,0:T(4,128)} broadcast(f32[64,64,4]{2,1,0:T(8,128)S(1)} %copy.183), dimensions={0,1,2} | broadcast | bytes 8454144 | tf_op jit(solution)/shard_map/broadcast_in_dim | solution.py:17
  127.3 10.3 %broadcast_in_dim.114 = f32[64,1,64,512]{3,2,0,1:T(8,128)} reshape(f32[64,64,4,128]{3,2,1,0:T(4,128)} %broadcast_in_dim.113) | data formatting | bytes 16777216 | tf_op jit(solution)/shard_map/broadcast_in_dim | solution.py:17
  137.6 178.8 %all-to-all-done.1 = bf16[64,1,64,576]{3,2,1,0:T(8,128)(2,1)} async-done(((bf16[64,1,64,576]{3,2,1,0:T(8,128)(2,1)}), bf16[64,1,64,576]{3,2,1,0:T(8,128)(2,1)}, u32[]{:S(2)}, u32[]{:S(2)}) %all-to-all-start.1) | async-done | bytes 4718624 | tf_op jit(solution)/shard_map/all_to_all | solution.py:66
  316.4 6.0 %gather_fusion.4 = bf16[64,64,576]{2,1,0:T(8,128)(2,1)} fusion(bf16[64,64,576]{2,1,0:T(8,128)(2,1)} %bitcast.15, s32[1024]{0:T(1024)S(1)} %pad_clamp_fusion.1), kind=kCustom, calls=%fused_computation.4 | custom fusion | bytes 9437440 | tf_op jit(solution)/shard_map/gather | solution.py:78
  322.4 1.3 slice_bitcast_fusion
  323.7 6.3 %fusion = bf16[64,64,512]{2,1,0:T(8,128)(2,1)S(1)} fusion(f32[64,1,64,512]{3,2,0,1:T(8,128)} %broadcast_in_dim.114, bf16[64,1,64,576]{3,2,0,1:T(8,128)(2,1)} %bitcast.120), kind=kLoop, calls=%fused_computation.9 | loop fusion | flops 6291456 | bytes 16777216 | tf_op jit(solution)/shard_map/concatenate | solution.py:20
  330.0 2.4 fusion.76
  332.5 2.4 fusion.74
  335.0 1.2 fusion.38
  337.5 3.1 fusion.41
  340.6 3.1 fusion.20
  343.8 0.7 reshape.267
  344.6 0.8 copy.193
  345.8 2.0 fusion.4
  348.1 2.9 fusion.42
  351.1 1.4 fusion.43
  352.4 3.8 %fusion.19 = bf16[64,8,128]{2,0,1:T(8,128)(2,1)S(1)} fusion(bf16[8,512,128]{2,1,0:T(8,128)(2,1)S(1)} %copy-done, bf16[1024,512,1]{1,0,2:T(8,128)(2,1)S(1)} %bitcast.123, f32[64,8,512]{2,1,0:T(8,128)} %fusion.43, f32[64,8,512]{2,1,0:T(8,128)S(1)} %fusion.42, f32[64,8,1024]{2,0,1:T(8,128)} %get-tuple-element.41, f32[64,8]{0,1:T(8,128)S(1)} %add_add_fusion, ...), kind=kOutput, calls=%fused_computation.38 | convolution fusion | flops 606404608 | bytes 6426624 | tf_op jit(solution)/shard_map/while/body/eval_jaxpr/rhc,hcv->rhv/dot_general | solution.py:155
  356.4 0.7 pad_maximum_fusion.15
  (101 shorter events, 12.0 us)
Async XLA Ops:
  6.5 334.0 %copy-start = (bf16[8,512,128]{2,1,0:T(8,128)(2,1)S(1)}, bf16[8,512,128]{2,1,0:T(8,128)(2,1)}, u32[]{:S(2)}) copy-start(bf16[8,512,128]{2,1,0:T(8,128)(2,1)} %param.23) | copy-start | bytes 3145732
  6.5 54.3 %all-gather.2.cloned.1.call-start = ((), (), s32[]{:S(2)}) async-start(), calls=%async_computation.3 | async-start | bytes 2949120 | tf_op jit(solution)/shard_map/all_gather | solution.py:62
  10.9 34.7 %all-to-all-start = ((s32[64,1,1]{2,1,0:T(1,128)}), s32[64,1,1]{2,1,0:T(1,128)S(1)}, u32[]{:S(2)}, u32[]{:S(2)}) async-start(s32[64,1,1]{2,1,0:T(1,128)} %copy.173), calls=%async_computation | async-start | bytes 65536 | tf_op jit(solution)/shard_map/all_to_all | solution.py:68
  45.7 29.7 %all-to-all-start.2 = ((bf16[64,2,128]{2,1,0:T(2,128)(2,1)}), bf16[64,2,128]{2,1,0:T(2,128)(2,1)S(1)}, u32[]{:S(2)}, u32[]{:S(2)}) async-start(bf16[64,2,128]{2,1,0:T(2,128)(2,1)} %reshape.343), calls=%async_computation.2 | async-start | bytes 65536 | tf_op jit(solution)/shard_map/all_to_all | solution.py:67
  75.4 6.3 %copy-start.17 = (s32[64,8]{0,1:T(8,128)S(1)}, s32[64,8]{0,1:T(8,128)}, u32[]{:S(2)}) copy-start(s32[64,8]{0,1:T(8,128)} %param.19) | copy-start | bytes 6148
  75.4 9.4 %copy-start.16 = (bf16[16,64,4]{1,2,0:T(4,128)(2,1)S(1)}, bf16[16,64,4]{1,2,0:T(4,128)(2,1)}, u32[]{:S(2)}) copy-start(bf16[16,64,4]{1,2,0:T(4,128)(2,1)} %param.18) | copy-start | bytes 24580
  75.4 241.0 %all-to-all-start.1 = ((bf16[64,1,64,576]{3,2,1,0:T(8,128)(2,1)}), bf16[64,1,64,576]{3,2,1,0:T(8,128)(2,1)}, u32[]{:S(2)}, u32[]{:S(2)}) async-start(bf16[64,1,64,576]{3,2,1,0:T(8,128)(2,1)} %bitcast.118), calls=%async_computation.1 | async-start | bytes 10485760 | tf_op jit(solution)/shard_map/all_to_all | solution.py:66
  93.8 6.9 %copy-start.2 = (bf16[16,64,512]{2,1,0:T(8,128)(2,1)}, bf16[16,64,512]{2,1,0:T(8,128)(2,1)S(1)}, u32[]{:S(2)}) copy-start(bf16[16,64,512]{2,1,0:T(8,128)(2,1)S(1)} %multiply_convert_fusion.1) | copy-start | bytes 3145732
  93.8 5.7 %copy-start.5 = (bf16[2,64,8,576]{3,2,1,0:T(8,128)(2,1)S(1)}, bf16[2,64,8,576]{3,2,1,0:T(8,128)(2,1)}, u32[]{:S(2)}) copy-start(bf16[2,64,8,576]{3,2,1,0:T(8,128)(2,1)} %param.21) | copy-start | bytes 3538948
  104.1 6.8 %copy-start.7 = (s32[64,1024]{1,0:T(8,128)S(1)}, s32[64,1024]{1,0:T(8,128)}, u32[]{:S(2)}) copy-start(s32[64,1024]{1,0:T(8,128)} %add.113) | copy-start | bytes 786436
  104.1 6.9 %copy-start.10 = (pred[64,1024]{1,0:T(8,128)(4,1)S(1)}, pred[64,1024]{1,0:T(8,128)(4,1)}, u32[]{:S(2)}) copy-start(pred[64,1024]{1,0:T(8,128)(4,1)} %and.28) | copy-start | bytes 196612
  111.8 3.9 %copy-start.8 = (bf16[1024,512]{0,1:T(8,128)(2,1)S(1)}, bf16[1024,512]{0,1:T(8,128)(2,1)}, u32[]{:S(2)}) copy-start(bf16[1024,512]{0,1:T(8,128)(2,1)} %copy.176) | copy-start | bytes 3145732
  111.8 3.9 %copy-start.12 = (bf16[1024,64]{0,1:T(8,128)(2,1)S(1)}, bf16[1024,64]{0,1:T(8,128)(2,1)}, u32[]{:S(2)}) copy-start(bf16[1024,64]{0,1:T(8,128)(2,1)} %copy.208) | copy-start | bytes 393220
  323.7 6.3 %copy-start.6 = (bf16[2,64,8,576]{3,2,1,0:T(8,128)(2,1)S(1)}, bf16[2,64,8,576]{3,2,1,0:T(8,128)(2,1)}, u32[]{:S(2)}) copy-start(bf16[2,64,8,576]{3,2,1,0:T(8,128)(2,1)} %param.21) | copy-start | bytes 3538948
  330.0 2.5 copy-start.1
  332.5 2.5 copy-start.15
  332.5 3.8 %copy-start.4 = (f32[64,8,1024]{2,0,1:T(8,128)S(1)}, f32[64,8,1024]{2,0,1:T(8,128)}, u32[]{:S(2)}) copy-start(f32[64,8,1024]{2,0,1:T(8,128)} %get-tuple-element.45) | copy-start | bytes 6291460
  337.5 3.1 copy-start.3
  340.6 4.8 %copy-start.18 = (f32[64,8]{0,1:T(8,128)S(1)}, f32[64,8]{0,1:T(8,128)}, u32[]{:S(2)}) copy-start(f32[64,8]{0,1:T(8,128)} %copy.196) | copy-start | bytes 6148
  340.6 4.8 %copy-start.19 = (f32[64,8]{0,1:T(8,128)S(1)}, f32[64,8]{0,1:T(8,128)}, u32[]{:S(2)}) copy-start(f32[64,8]{0,1:T(8,128)} %get-tuple-element.40) | copy-start | bytes 6148
  343.7 4.1 %copy-start.13 = (f32[64,8,2]{1,2,0:T(2,128)S(1)}, f32[64,8,2]{1,2,0:T(2,128)}, u32[]{:S(2)}) copy-start(f32[64,8,2]{1,2,0:T(2,128)} %get-tuple-element.38) | copy-start | bytes 12292
  348.1 3.0 copy-start.11
  348.1 3.0 copy-start.14
  352.4 4.0 %copy-start.9 = (bf16[1,64,1024]{2,1,0:T(8,128)(2,1)S(1)}, bf16[1,64,1024]{2,1,0:T(8,128)(2,1)}, u32[]{:S(2)}) copy-start(bf16[1,64,1024]{2,1,0:T(8,128)(2,1)} %reshape.267) | copy-start | bytes 393220
Sparse Core Ops, SparseCore 0:
  9.5 37.5 all-gather.1
where the time goes:
time: 365 us; the launch traced here: 364 us
  waiting for transfers between devices  189 us (52%)
  local copies, waits for them, and re-layouts  58.3 us (16%)
  starting transfers between devices  40.2 us (11%)
  matrix products  29.1 us (8%)
  other arithmetic  20.6 us (6%)
  between operations  13.8 us (4%)
  blocking collectives  13 us (4%)
    all_to_all x1, waiting for transfers between devices, shards(): lax.all_to_all(full_codes[slot_pages], 'inst', split_axis=0, concat_axis=...  179 us
    broadcast_in_dim x3, local copies, waits for them, and re-layouts, dequantize(): spread_rows = jnp.repeat(tile_scales.astype(jnp.float32), TILE, axis=-1)  19.6 us
    all_to_all x1, starting transfers between devices, shards(): lax.all_to_all(slot_lengths, 'inst', split_axis=0, concat_axis=0, tiled=T...  18.7 us
    all_to_all x1, starting transfers between devices, shards(): lax.all_to_all(full_scales[slot_pages], 'inst', split_axis=0, concat_axis...  15.1 us
    all_gather x1, blocking collectives, shards(): lax.all_gather(prefill_scales, 'head', axis=1, tiled=True)  13 us
    all_to_all x1, waiting for transfers between devices, shards(): lax.all_to_all(full_scales[slot_pages], 'inst', split_axis=0, concat_axis...  9.32 us
  transfers between devices with their start and end apart: 4, of which 2 were waited for; matrix products, arithmetic and copies ran while one was open for 19% of the time, Pallas kernels for 0%

commit v1 on v0

--- a/solution.py
+++ b/solution.py
@@ -58,15 +58,12 @@
     slot_lengths = jnp.where(present, req_lengths[chosen], 0)
     pool_keys = dequantize(pool_codes, pool_scales)
     flattened_pool = pool_keys.reshape(pool_pages * page_size, width)
-    full_codes, full_scales = (
-        lax.all_gather(prefill_codes, "head", axis=1, tiled=True),
-        lax.all_gather(prefill_scales, "head", axis=1, tiled=True),
-    )
-    recv_codes, recv_scales, recv_lengths = (
-        lax.all_to_all(full_codes[slot_pages], "inst", split_axis=0, concat_axis=0, tiled=True),
-        lax.all_to_all(full_scales[slot_pages], "inst", split_axis=0, concat_axis=0, tiled=True),
+    pref_keys = dequantize(prefill_codes, prefill_scales)
+    recv_keys, recv_lengths = (
+        lax.all_to_all(pref_keys[slot_pages[:, 0]], "inst", split_axis=0, concat_axis=0, tiled=True),
         lax.all_to_all(slot_lengths, "inst", split_axis=0, concat_axis=0, tiled=True),
     )
+    recv_keys = lax.all_gather(recv_keys, "head", axis=1, tiled=True)
     present_src = (recv_lengths > 0).astype(jnp.int32)
     slot_rank = jnp.cumsum(present_src) - 1
     arrivals = jnp.sum(present_src)
@@ -75,7 +72,7 @@
     anchor = jnp.sum(picked.astype(jnp.int32) * group_ids[None, :], axis=1)
     arrived = row_ids < arrivals
     arr_len = jnp.where(arrived, recv_lengths[anchor], 0)
-    arr_keys = dequantize(recv_codes[anchor], recv_scales[anchor]).reshape(row_count, -1, width)
+    arr_keys = recv_keys[anchor]
     arr_mask = jnp.arange(arr_keys.shape[1], dtype=jnp.int32)[None, :] < arr_len[:, None]
     table_hit = res_tables[:, :, None] == jnp.arange(pool_pages, dtype=jnp.int32)[None, None, :]
     listed = jnp.any(table_hit, axis=1)

time: 365 us -> 157 us (0.43)
  the two profiles are of different devices: /device:TPU:2 before, /device:TPU:1 now
where the time goes in v1:
time: 157 us; the launch traced here: 156 us
  blocking collectives  54.1 us (34%)
  matrix products  32.5 us (21%)
  local copies, waits for them, and re-layouts  30.9 us (20%)
  other arithmetic  15.9 us (10%)
  between operations  13.7 us (9%)
  starting transfers between devices  9.12 us (6%)
    all_to_all x1, blocking collectives, shards(): lax.all_to_all(pref_keys[slot_pages[:, 0]], 'inst', split_axis=0, concat_...  54.1 us
    all_to_all x1, starting transfers between devices, shards(): lax.all_to_all(slot_lengths, 'inst', split_axis=0, concat_axis=0, tiled=T...  9.12 us
    dot_general x2, matrix products, run_block(): jnp.einsum('rhc,hcv->rhv', latent_state, value_projection, preferred_elem...  7.56 us
    dot_general x2, matrix products, run_block(): jnp.einsum('rhc,rkc->rhk', step_query, block_arriving, preferred_element_...  7.51 us
    dot_general x2, matrix products, run_block(): jnp.einsum(score_form, step_query, flattened_pool, preferred_element_type...  6.24 us
    gather x1, local copies, waits for them, and re-layouts, shards(): arr_keys = recv_keys[anchor]  6.01 us
    dot_general x2, matrix products, run_block(): jnp.einsum('luy,lyb->lub', arr_weights, arriving_latent, preferred_elemen...  5.85 us
    reduce_sum x2, other arithmetic, run_block(): jnp.sum(res_exp, axis=-1, keepdims=True)  4.09 us
  transfers between devices with their start and end apart: 2, of which 0 were waited for; matrix products, arithmetic and copies ran while one was open for 23% of the time, Pallas kernels for 0%

profile of v1, /device:TPU:1, one launch (start us, length us, event | category | flops | bytes accessed | tf_op | source)
XLA Modules:
  0.0 156.2 jit_solution(4102259962505453247)
XLA Ops:
  6.5 0.8 select_reduce_fusion.2
  7.4 1.4 gather_fusion.2
  8.8 0.8 copy.135
  9.6 0.8 slice.44
  10.5 1.2 fusion.33
  11.7 0.7 gather_fusion.3
  12.4 54.1 %all_to_all.14 = bf16[64,8,576]{2,1,0:T(8,128)(2,1)} all-to-all(bf16[64,8,576]{2,1,0:T(8,128)(2,1)S(1)} %gather_fusion.3), channel_id=1, replica_groups=mesh['inst'=64,'head'=8] {'inst'}, dimensions={0} | all-to-all | bytes 1179648 | tf_op jit(solution)/shard_map/all_to_all | solution.py:63
  66.5 0.8 gather_fusion
  67.4 0.7 copy.129
  68.1 9.1 %all-to-all-start = ((s32[64,1,1]{2,1,0:T(1,128)}), s32[64,1,1]{2,1,0:T(1,128)}, u32[]{:S(2)}, u32[]{:S(2)}) async-start(s32[64,1,1]{2,1,0:T(1,128)} %copy.129), calls=%async_computation | async-start | bytes 65536 | tf_op jit(solution)/shard_map/all_to_all | solution.py:64
  77.2 1.0 copy.130
  78.2 2.2 %broadcast_in_dim.106 = f32[16,64,4,128]{3,2,1,0:T(4,128)S(1)} broadcast(f32[16,64,4]{2,1,0:T(8,128)} %copy.130), dimensions={0,1,2} | broadcast | bytes 2113536 | tf_op jit(solution)/shard_map/broadcast_in_dim | solution.py:17
  80.5 1.9 %reshape.230 = f32[16,64,512]{2,1,0:T(8,128)} reshape(f32[16,64,4,128]{3,2,1,0:T(4,128)S(1)} %broadcast_in_dim.106) | data formatting | bytes 4194304 | tf_op jit(solution)/shard_map/reshape | solution.py:17
  82.4 1.0 slice_bitcast_fusion
  83.5 0.7 fusion.47
  84.1 2.2 %fusion.31 = f32[64,1,8]{2,1,0:T(1,128)} fusion(bf16[64,576,1]{1,0,2:T(8,128)(2,1)S(1)} %get-tuple-element.26, bf16[2,64,8,576]{3,2,1,0:T(8,128)(2,1)} %param.21), kind=kOutput, calls=%fused_computation.47 | convolution fusion | flops 589824 | bytes 731136 | tf_op jit(solution)/shard_map/while/body/eval_jaxpr/rhc,rjc->rhj/dot_general | solution.py:114
  86.3 1.8 %fusion.67 = (f32[64,8]{1,0:T(8,128)}, f32[64,8,2]{1,2,0:T(2,128)}) fusion(bf16[2,64,576]{2,1,0:T(8,128)(2,1)S(1)} %copy-done.11, bf16[2,64,8,576]{3,2,1,0:T(8,128)(2,1)S(1)} %copy-done.4), kind=kOutput, calls=%fused_computation.126 | convolution fusion | flops 1181184 | bytes 825344 | tf_op jit(solution)/shard_map/while/body/eval_jaxpr/rhc,rjc->rhj/dot_general | solution.py:114
  88.1 1.2 fusion.66
  89.8 0.8 slice.41
  90.5 0.8 copy.191
  91.4 1.0 add.108
  92.4 1.9 %add.109 = s32[64,1024]{1,0:T(8,128)} reshape(s32[64,16,64]{2,1,0:T(8,128)} %add.108) | data formatting | bytes 524288 | tf_op jit(solution)/shard_map/add | solution.py:84
  94.6 0.8 and.28
  95.5 1.3 copy.132
  96.8 1.7 %copy.160 = bf16[1024,64]{0,1:T(8,128)(2,1)} copy(bf16[1024,64]{1,0:T(8,128)(2,1)} %bitcast.107) | data formatting | bytes 262144 | tf_op jit(solution)/shard_map/concatenate | solution.py:20
  98.7 0.8 compare_convert_fusion
  99.6 2.0 %reduce = s32[64]{0:T(128)S(1)} reduce(s32[64,1,1]{2,1,0:T(1,128)} %all-to-all-done, s32[]{:T(128)} %constant.22.clone.1), dimensions={1,2}, to_apply=%all_to_all.9.reduce_sub_computation | reduce | bytes 516 | tf_op jit(solution)/shard_map/all_to_all | solution.py:64
  101.9 0.8 gather_fusion.1
  102.6 0.6 fusion.59
  103.3 0.7 compare_not_fusion
  103.9 0.7 compare_select_fusion.3
  104.7 1.1 fusion.37
  105.8 3.9 %fusion.70 = (f32[64,8]{0,1:T(8,128)S(1)}, f32[64,8,1024]{2,0,1:T(8,128)}) fusion(bf16[1,64,8,576]{3,2,1,0:T(8,128)(2,1)} %get-tuple-element.23, bf16[1024,64]{0,1:T(8,128)(2,1)} %copy.160, bf16[1024,512]{0,1:T(8,128)(2,1)} %copy.132, pred[64,1024]{1,0:T(8,128)(4,1)S(1)} %fusion.37), kind=kOutput, calls=%fused_computation.129 | convolution fusion | flops 607911424 | bytes 3934208 | tf_op jit(solution)/shard_map/while/body/eval_jaxpr/rhc,kc->rhk/dot_general | solution.py:102
  109.8 2.3 %fusion.68 = (f32[64,8]{0,1:T(8,128)S(1)}, f32[64,8,1024]{2,0,1:T(8,128)}) fusion(bf16[1,64,8,576]{3,2,1,0:T(8,128)(2,1)S(1)} %copy-done.9, bf16[1024,64]{0,1:T(8,128)(2,1)S(1)} %copy-done.14, bf16[1024,512]{0,1:T(8,128)(2,1)S(1)} %copy-done.8, pred[64,1024]{1,0:T(8,128)(4,1)S(1)} %fusion.37), kind=kOutput, calls=%fused_computation.127 | convolution fusion | flops 607911424 | bytes 3934208 | tf_op jit(solution)/shard_map/while/body/eval_jaxpr/rhc,kc->rhk/dot_general | solution.py:102
  112.1 6.0 %gather_fusion.4 = bf16[64,64,576]{2,1,0:T(8,128)(2,1)} fusion(bf16[64,64,576]{2,1,0:T(8,128)(2,1)} %all-gather.2.cloned.1.call-done, s32[1024]{0:T(1024)S(1)} %pad_clamp_fusion.1), kind=kCustom, calls=%fused_computation.4 | custom fusion | bytes 9437440 | tf_op jit(solution)/shard_map/gather | solution.py:75
  118.1 5.1 %fusion.71 = (f32[64,8]{1,0:T(8,128)S(1)}, f32[64,8,64]{2,1,0:T(8,128)}) fusion(bf16[64,64,576]{2,1,0:T(8,128)(2,1)} %gather_fusion.4, bf16[2,64,8,576]{3,2,1,0:T(8,128)(2,1)S(1)} %copy-done.4, pred[64,64]{1,0:T(8,128)(4,1)S(1)} %iota_compare_fusion.2), kind=kOutput, calls=%fused_computation.130 | convolution fusion | flops 37846528 | bytes 5515264 | tf_op jit(solution)/shard_map/while/body/eval_jaxpr/rhc,rkc->rhk/dot_general | solution.py:108
  123.1 2.4 %fusion.69 = (f32[64,8]{1,0:T(8,128)S(1)}, f32[64,8,64]{2,1,0:T(8,128)}) fusion(bf16[64,64,576]{2,1,0:T(8,128)(2,1)S(1)} %copy-done.2, bf16[2,64,8,576]{3,2,1,0:T(8,128)(2,1)S(1)} %copy-done.4, pred[64,64]{1,0:T(8,128)(4,1)S(1)} %iota_compare_fusion.2), kind=kOutput, calls=%fused_computation.128 | convolution fusion | flops 37846528 | bytes 6039552 | tf_op jit(solution)/shard_map/while/body/eval_jaxpr/rhc,rkc->rhk/dot_general | solution.py:108
  125.7 1.2 fusion.38
  127.0 2.0 %fusion.4 = f32[64,8]{0,1:T(8,128)S(1)} fusion(f32[64,8,1024]{2,0,1:T(8,128)} %get-tuple-element.45, f32[64,8]{0,1:T(8,128)S(1)} %maximum_maximum_fusion.1), kind=kLoop, calls=%fused_computation.16 | loop fusion | flops 1048064 | bytes 2101248 | tf_op jit(solution)/shard_map/while/body/eval_jaxpr/reduce_sum | solution.py:132
  129.2 2.9 %fusion.2 = f32[64,8,512]{2,1,0:T(8,128)S(1)} fusion(bf16[64,64,576]{2,1,0:T(8,128)(2,1)} %gather_fusion.4, f32[64,8,64]{2,1,0:T(8,128)S(1)} %copy-done.6, f32[64,8]{1,0:T(8,128)S(1)} %copy.140, f32[64,8]{1,0:T(8,128)S(1)} %copy.138), kind=kOutput, calls=%fused_computation.7 | convolution fusion | flops 33652736 | bytes 5378048 | tf_op jit(solution)/shard_map/while/body/eval_jaxpr/luy,lyb->lub/dot_general | solution.py:142
  132.1 3.7 %fusion.19 = bf16[64,8,128]{2,0,1:T(8,128)(2,1)} fusion(bf16[8,512,128]{2,1,0:T(8,128)(2,1)S(1)} %copy-done, bf16[1024,512,1]{1,0,2:T(8,128)(2,1)S(1)} %bitcast.105, f32[64,8,512]{2,1,0:T(8,128)S(1)} %fusion.2, f32[64,8,1024]{2,0,1:T(8,128)} %get-tuple-element.45, f32[64,8]{0,1:T(8,128)S(1)} %get-tuple-element.22, f32[64,8]{0,1:T(8,128)S(1)} %maximum_maximum_fusion.1, ...), kind=kOutput, calls=%fused_computation.36 | convolution fusion | flops 606666752 | bytes 5511168 | tf_op jit(solution)/shard_map/while/body/eval_jaxpr/rhc,hcv->rhv/dot_general | solution.py:152
  135.8 1.0 copy.142
  136.8 0.7 reshape.234
  138.0 2.0 %fusion.5 = f32[64,8]{0,1:T(8,128)S(1)} fusion(f32[64,8,1024]{2,0,1:T(8,128)} %get-tuple-element.41, f32[64,8]{0,1:T(8,128)S(1)} %maximum_maximum_fusion), kind=kLoop, calls=%fused_computation.17 | loop fusion | flops 1048064 | bytes 2101248 | tf_op jit(solution)/shard_map/while/body/eval_jaxpr/reduce_sum | solution.py:132
  140.4 2.9 %fusion = f32[64,8,512]{2,1,0:T(8,128)S(1)} fusion(bf16[64,64,576]{2,1,0:T(8,128)(2,1)} %gather_fusion.4, f32[64,8,64]{2,1,0:T(8,128)S(1)} %copy-done.5, f32[64,8]{1,0:T(8,128)S(1)} %copy.153, f32[64,8]{1,0:T(8,128)S(1)} %copy.149), kind=kOutput, calls=%fused_computation.5 | convolution fusion | flops 33652736 | bytes 5378048 | tf_op jit(solution)/shard_map/while/body/eval_jaxpr/luy,lyb->lub/dot_general | solution.py:142
  143.3 1.4 fusion.41
  144.7 3.8 %fusion.18 = bf16[64,8,128]{2,0,1:T(8,128)(2,1)S(1)} fusion(bf16[8,512,128]{2,1,0:T(8,128)(2,1)S(1)} %copy-done, bf16[1024,512,1]{1,0,2:T(8,128)(2,1)S(1)} %bitcast.106, f32[64,8,512]{2,1,0:T(8,128)} %fusion.41, f32[64,8,512]{2,1,0:T(8,128)S(1)} %fusion, f32[64,8,1024]{2,0,1:T(8,128)} %get-tuple-element.41, f32[64,8]{0,1:T(8,128)S(1)} %add_add_fusion, ...), kind=kOutput, calls=%fused_computation.35 | convolution fusion | flops 606404608 | bytes 6426624 | tf_op jit(solution)/shard_map/while/body/eval_jaxpr/rhc,hcv->rhv/dot_general | solution.py:152
  148.7 0.7 pad_maximum_fusion.1
  (88 shorter events, 2.9 us)
Async XLA Ops:
  6.5 125.5 %copy-start = (bf16[8,512,128]{2,1,0:T(8,128)(2,1)S(1)}, bf16[8,512,128]{2,1,0:T(8,128)(2,1)}, u32[]{:S(2)}) copy-start(bf16[8,512,128]{2,1,0:T(8,128)(2,1)} %param.23) | copy-start | bytes 3145732
  6.5 105.5 %all-gather.2.cloned.1.call-start = ((), (), s32[]{:S(2)}) async-start(), calls=%async_computation.2 | async-start | bytes 5898240 | tf_op jit(solution)/shard_map/all_gather | solution.py:66
  11.6 54.9 %copy-start.1 = (s32[32]{0:T(128)S(1)}, s32[32]{0:T(128)}, u32[]{:S(2)}) copy-start(s32[32]{0:T(128)} %param.15) | copy-start | bytes 388
  11.7 55.7 %copy-start.20 = (s32[32]{0:T(128)S(1)}, s32[32]{0:T(128)}, u32[]{:S(2)}) copy-start(s32[32]{0:T(128)} %param.16) | copy-start | bytes 388
  11.7 65.5 %copy-start.18 = (bf16[16,64,4]{1,2,0:T(4,128)(2,1)S(1)}, bf16[16,64,4]{1,2,0:T(4,128)(2,1)}, u32[]{:S(2)}) copy-start(bf16[16,64,4]{1,2,0:T(4,128)(2,1)} %param.18) | copy-start | bytes 24580
  68.1 30.6 %all-to-all-start = ((s32[64,1,1]{2,1,0:T(1,128)}), s32[64,1,1]{2,1,0:T(1,128)}, u32[]{:S(2)}, u32[]{:S(2)}) async-start(s32[64,1,1]{2,1,0:T(1,128)} %copy.129), calls=%async_computation | async-start | bytes 65536 | tf_op jit(solution)/shard_map/all_to_all | solution.py:64
  80.5 1.9 %copy-start.19 = (s32[64,8]{0,1:T(8,128)S(1)}, s32[64,8]{0,1:T(8,128)}, u32[]{:S(2)}) copy-start(s32[64,8]{0,1:T(8,128)} %param.19) | copy-start | bytes 6148
  82.4 3.9 %copy-start.4 = (bf16[2,64,8,576]{3,2,1,0:T(8,128)(2,1)S(1)}, bf16[2,64,8,576]{3,2,1,0:T(8,128)(2,1)}, u32[]{:S(2)}) copy-start(bf16[2,64,8,576]{3,2,1,0:T(8,128)(2,1)} %param.21) | copy-start | bytes 3538948
  82.4 3.9 %copy-start.11 = (bf16[2,64,576]{2,1,0:T(8,128)(2,1)S(1)}, bf16[2,64,576]{2,1,0:T(8,128)(2,1)}, u32[]{:S(2)}) copy-start(bf16[2,64,576]{2,1,0:T(8,128)(2,1)} %param.22) | copy-start | bytes 442372
  86.3 3.0 %copy-start.3 = (f32[16,64,512]{2,1,0:T(8,128)S(1)}, f32[16,64,512]{2,1,0:T(8,128)}, u32[]{:S(2)}) copy-start(f32[16,64,512]{2,1,0:T(8,128)} %reshape.230) | copy-start | bytes 6291460
  86.3 3.0 %copy-start.7 = (bf16[16,64,576]{2,1,0:T(8,128)(2,1)S(1)}, bf16[16,64,576]{2,1,0:T(8,128)(2,1)}, u32[]{:S(2)}) copy-start(bf16[16,64,576]{2,1,0:T(8,128)(2,1)} %param.17) | copy-start | bytes 3538948
  95.4 3.1 %copy-start.16 = (f32[64,1,8]{2,1,0:T(1,128)S(1)}, f32[64,1,8]{2,1,0:T(1,128)}, u32[]{:S(2)}) copy-start(f32[64,1,8]{2,1,0:T(1,128)} %fusion.31) | copy-start | bytes 6148
  95.4 3.2 %copy-start.17 = (f32[64,8]{1,0:T(8,128)S(1)}, f32[64,8]{1,0:T(8,128)}, u32[]{:S(2)}) copy-start(f32[64,8]{1,0:T(8,128)} %get-tuple-element.36) | copy-start | bytes 6148
  95.4 9.2 %copy-start.12 = (pred[64,1024]{1,0:T(8,128)(4,1)S(1)}, pred[64,1024]{1,0:T(8,128)(4,1)}, u32[]{:S(2)}) copy-start(pred[64,1024]{1,0:T(8,128)(4,1)} %and.28) | copy-start | bytes 196612
  105.8 4.0 %copy-start.8 = (bf16[1024,512]{0,1:T(8,128)(2,1)S(1)}, bf16[1024,512]{0,1:T(8,128)(2,1)}, u32[]{:S(2)}) copy-start(bf16[1024,512]{0,1:T(8,128)(2,1)} %copy.132) | copy-start | bytes 3145732
  105.8 4.0 %copy-start.9 = (bf16[1,64,8,576]{3,2,1,0:T(8,128)(2,1)S(1)}, bf16[1,64,8,576]{3,2,1,0:T(8,128)(2,1)}, u32[]{:S(2)}) copy-start(bf16[1,64,8,576]{3,2,1,0:T(8,128)(2,1)} %get-tuple-element.24) | copy-start | bytes 1769476
  105.8 4.0 %copy-start.14 = (bf16[1024,64]{0,1:T(8,128)(2,1)S(1)}, bf16[1024,64]{0,1:T(8,128)(2,1)}, u32[]{:S(2)}) copy-start(bf16[1024,64]{0,1:T(8,128)(2,1)} %copy.160) | copy-start | bytes 393220
  118.1 5.1 %copy-start.2 = (bf16[64,64,576]{2,1,0:T(8,128)(2,1)S(1)}, bf16[64,64,576]{2,1,0:T(8,128)(2,1)}, u32[]{:S(2)}) copy-start(bf16[64,64,576]{2,1,0:T(8,128)(2,1)} %gather_fusion.4) | copy-start | bytes 14155780
  125.6 3.6 %copy-start.6 = (f32[64,8,64]{2,1,0:T(8,128)S(1)}, f32[64,8,64]{2,1,0:T(8,128)}, u32[]{:S(2)}) copy-start(f32[64,8,64]{2,1,0:T(8,128)} %get-tuple-element.47) | copy-start | bytes 393220
  132.1 5.6 %copy-start.5 = (f32[64,8,64]{2,1,0:T(8,128)S(1)}, f32[64,8,64]{2,1,0:T(8,128)}, u32[]{:S(2)}) copy-start(f32[64,8,64]{2,1,0:T(8,128)} %get-tuple-element.43) | copy-start | bytes 393220
  135.8 4.3 %copy-start.15 = (f32[64,8,2]{1,2,0:T(2,128)S(1)}, f32[64,8,2]{1,2,0:T(2,128)}, u32[]{:S(2)}) copy-start(f32[64,8,2]{1,2,0:T(2,128)} %get-tuple-element.38) | copy-start | bytes 12292
  140.4 3.0 %copy-start.13 = (bf16[2,64,576]{2,0,1:T(2,128)(2,1)S(1)}, bf16[2,64,576]{2,0,1:T(2,128)(2,1)}, u32[]{:S(2)}) copy-start(bf16[2,64,576]{2,0,1:T(2,128)(2,1)} %copy.191) | copy-start | bytes 442372
  144.7 4.0 %copy-start.10 = (bf16[1,64,1024]{2,1,0:T(8,128)(2,1)S(1)}, bf16[1,64,1024]{2,1,0:T(8,128)(2,1)}, u32[]{:S(2)}) copy-start(bf16[1,64,1024]{2,1,0:T(8,128)(2,1)} %reshape.234) | copy-start | bytes 393220
Sparse Core Ops, SparseCore 0:
  66.6 39.9 all-gather.1

commit v2 on v1

v2 whole, which is shorter than its diff:
```python
import functools
import math

import jax
import jax.numpy as jnp
from jax import lax
from jax.experimental import pallas as pl
from jax.experimental.pallas import tpu as pltpu
from jax.sharding import PartitionSpec as P

LATENT_WIDTH = 512
LAT = 576
WIDE = 640
NZ, NY, NX = 16, 4, 4
SLOTS = NZ * NY // 2
CHUNKS = SLOTS // 4
BIG = 1e30
MESH = pl.DeviceIdType.MESH
softmax_scale = (0.1 * math.log(40.0) + 1.0) ** 2 / math.sqrt(192.0)
F32, BF16, I32 = jnp.float32, jnp.bfloat16, jnp.int32


def iota(shape, axis):
    return lax.broadcasted_iota(I32, shape, axis)


def dot(a, b):
    return lax.dot_general(a, b, (((1,), (0,)), ((), ())), preferred_element_type=F32)


def dot_t(a, b):
    return lax.dot_general(a, b, (((1,), (1,)), ((), ())), preferred_element_type=F32)


def slot_offset(m, core):
    q, sign, half = m // 4, (m // 2) % 2, m % 2
    if isinstance(m, int):
        dz = q if sign == 0 else (NZ - q if q else NZ // 2)
    else:
        dz = jnp.where(sign == 0, q, jnp.where(q == 0, NZ // 2, NZ - q))
    return dz, 2 * half + core


def dequantize_into(dst, codes, scales, rows, start):
    for tile in range(4):
        lanes = slice(tile * 128, tile * 128 + 128)
        dst[start : start + rows, lanes] = (
            codes[:, lanes].astype(F32) * scales[:, tile : tile + 1].astype(F32)
        ).astype(BF16)
    dst[start : start + rows, 512:LAT] = codes[:, 512:LAT]


def softmax_mix(scores, fresh_scores, values, fresh_values):
    scores = scores * softmax_scale
    fresh_scores = fresh_scores * softmax_scale
    highest = jnp.maximum(
        jnp.max(scores, axis=1, keepdims=True), jnp.max(fresh_scores, axis=1, keepdims=True)
    )
    weights = jnp.exp(scores - highest)
    fresh_weights = jnp.exp(fresh_scores - highest)
    total = jnp.sum(weights, axis=1, keepdims=True) + jnp.sum(fresh_weights, axis=1, keepdims=True)
    mixed = dot(weights.astype(BF16), values) + dot(fresh_weights.astype(BF16), fresh_values)
    return (mixed / total).astype(BF16)


def kernel(
    codes, scales, pages, lengths, dests, pool_codes, pool_scales, tables, res_lengths,
    queries, fresh, projection, out,
    keys, packed, pages_in, res_keys, wide_q, slot_q, slot_fresh, slot_lat, lat,
    key_send, key_recv, a_send, a_recv, r_send, r_recv, l_send, l_recv,
    rr_send, rr_recv, ll_send, ll_recv, p_send, p_recv, own_sem,
):
    inst, head = lax.axis_index("inst"), lax.axis_index("head")
    z, y = inst // NY, inst % NY
    x, core = head // 2, head % 2
    right_x, left_x, far_x = (x + 1) % NX, (x + NX - 1) % NX, (x + 2) % NX
    right, left = (inst, right_x * 2 + core), (inst, left_x * 2 + core)
    partner = (inst, x * 2 + 1 - core)

    def target(m):
        dz, dy = slot_offset(m, core)
        return (((z + dz) % NZ) * NY + (y + dy) % NY, head)

    barrier = pltpu.get_barrier_semaphore()
    for device in (partner, right, left):
        pl.semaphore_signal(barrier, inc=1, device_id=device, device_id_type=MESH)
    for m in range(SLOTS):
        if m == 0:
            @pl.when(core == 1)
            def _():
                pl.semaphore_signal(barrier, inc=1, device_id=target(0), device_id_type=MESH)
        else:
            pl.semaphore_signal(barrier, inc=1, device_id=target(m), device_id_type=MESH)

    own = keys.at[core]
    own[:, 512:WIDE] = jnp.zeros((256, 128), BF16)
    dequantize_into(own, codes, scales, 256, 0)

    pl.semaphore_wait(barrier, SLOTS + 2 + core)
    key_copy = pltpu.make_async_remote_copy(
        src_ref=own, dst_ref=own, send_sem=key_send, recv_sem=key_recv,
        device_id=partner, device_id_type=MESH,
    )
    key_copy.start()

    rows = SLOTS * 16
    row = iota((rows, 32), 0)
    dz, dy = slot_offset(row // 16, core)
    wanted = ((z + dz) % NZ) * NY + (y + dy) % NY
    hit = dests[...] == wanted
    page = jnp.sum(jnp.where(hit, pages[...].astype(F32) + 1.0, 0.0), axis=1, keepdims=True)
    count = jnp.sum(jnp.where(hit, lengths[...].astype(F32), 0.0), axis=1, keepdims=True)
    slot_row = iota((rows, 1), 0)
    token = slot_row % 16
    column = (token // 8) * 256 + (page.astype(I32) - 1) * 8 + token % 8
    column = jnp.where(page > 0.5, column, -1)
    choose = jnp.where(column == iota((rows, 512), 1), 1.0, 0.0).astype(BF16)
    valid = (x * 16 + token).astype(F32) < count
    lane = iota((rows, 128), 1)
    mine = (lane - 64) == (slot_row // 16) % 4
    bias = jnp.where(lane < 68, jnp.where(mine & valid, 0.0, -BIG), 0.0)

    key_copy.wait()
    both = keys[...].reshape(512, WIDE)
    for tile in range(4):
        lanes = slice(tile * 128, tile * 128 + 128)
        packed[:, :, lanes] = dot(choose, both[:, lanes]).astype(BF16).reshape(SLOTS, 16, 128)
    last = dot(choose, both[:, 512:WIDE])
    packed[:, :, 512:WIDE] = jnp.where(lane < 64, last, bias).astype(BF16).reshape(SLOTS, 16, 128)

    def a_copy(m):
        return pltpu.make_async_remote_copy(
            src_ref=packed.at[m], dst_ref=pages_in.at[core, m // 4, x, m % 4],
            send_sem=a_send.at[m], recv_sem=a_recv.at[m],
            device_id=target(m), device_id_type=MESH,
        )

    own_copy = pltpu.make_async_copy(packed.at[0], pages_in.at[core, 0, x, 0], own_sem)
    order = list(range(1, CHUNKS)) + [0]
    for q in order:
        for m in range(4 * q, 4 * q + 4):
            if m == 0:
                pl.when(core == 1)(lambda: a_copy(0).start())
                pl.when(core == 0)(lambda: own_copy.start())
            else:
                a_copy(m).start()

    def resident_keys():
        listed = jnp.zeros((128, 16), F32)
        page_ids = iota((64, 16), 1)
        for j in range(8):
            left_over = jnp.clip(res_lengths[...].astype(F32) - 64.0 * j, 0.0, 64.0)
            part = jnp.where(tables[:, j : j + 1] == page_ids, left_over, 0.0)
            listed = listed + jnp.concatenate([part, part], axis=0)
        spread = jnp.where(iota((1024, 16), 0) // 64 == iota((1024, 16), 1), 1.0, 0.0).astype(BF16)
        held = dot_t(spread, listed.astype(BF16))
        place = (iota((1024, 128), 0) % 64).astype(F32)
        res_keys[0:1024, 512:WIDE] = jnp.where(place < held, 0.0, -BIG).astype(BF16)
        dequantize_into(res_keys, pool_codes, pool_scales, 1024, 0)
        same = iota((128, 128), 0) % 64 == iota((128, 128), 1) - 64
        res_keys[1024:1152, 512:WIDE] = jnp.where(same, 0.0, -BIG).astype(BF16)
        res_keys[1024:1152, 0:LAT] = fresh[...]
        row_of = (iota((1024, 128), 0) // 8) % 64
        wide_q[:, 512:WIDE] = jnp.where(row_of == iota((1024, 128), 1) - 64, 1.0, 0.0).astype(BF16)
        wide_q[:, 0:LAT] = queries[...]

    def resident_block(block):
        rows_at = slice(block * 128, block * 128 + 128)
        query = wide_q[rows_at, :]
        scores = dot_t(query, res_keys[0:1024, :])
        fresh_scores = dot_t(query, res_keys[1024:1152, :])
        if block < 4:
            fresh_scores = jnp.where(iota((128, 128), 1) < 64, fresh_scores, -BIG)
        mixed = softmax_mix(
            scores, fresh_scores, res_keys[0:1024, 0:512], res_keys[1024:1152, 0:512]
        ).astype(F32)
        for tile in range(4):
            lat[tile, rows_at, :] = mixed[:, tile * 128 : tile * 128 + 128]

    def hop(src_x, piece, q, sems, device):
        send, recv = sems
        ref = pages_in.at[core, q, src_x, piece]
        return pltpu.make_async_remote_copy(
            src_ref=ref, dst_ref=ref, send_sem=send.at[q], recv_sem=recv.at[q],
            device_id=device, device_id_type=MESH,
        )

    def to_partner(src_x, q, which, from_core):
        ref = pages_in.at[from_core, q, src_x]
        return pltpu.make_async_remote_copy(
            src_ref=ref, dst_ref=ref, send_sem=p_send.at[q, which], recv_sem=p_recv.at[q, which],
            device_id=partner, device_id_type=MESH,
        )

    whole, first, second = pl.ds(0, 4), pl.ds(0, 2), pl.ds(2, 2)
    right_sems, left_sems = (r_send, r_recv), (l_send, l_recv)
    far_right, far_left = (rr_send, rr_recv), (ll_send, ll_recv)

    def stage_own(q):
        for m in range(4 * q, 4 * q + 4):
            if m == 0:
                pl.when(core == 1)(lambda: a_copy(0).wait_recv())
                pl.when(core == 0)(lambda: own_copy.wait())
            else:
                a_copy(m).wait_recv()
        hop(x, whole, q, right_sems, right).start()
        hop(x, whole, q, left_sems, left).start()
        to_partner(x, q, 0, core).start()

    def stage_near(q):
        hop(left_x, whole, q, right_sems, right).wait_recv()
        hop(left_x, first, q, far_right, right).start()
        to_partner(left_x, q, 1, core).start()
        hop(right_x, whole, q, left_sems, left).wait_recv()
        hop(right_x, second, q, far_left, left).start()
        to_partner(right_x, q, 2, core).start()

    def stage_far(q):
        hop(far_x, first, q, far_right, right).wait_recv()
        hop(far_x, second, q, far_left, left).wait_recv()
        to_partner(far_x, q, 3, core).start()

    def stage_done(q):
        for which, src_x in enumerate((x, left_x, right_x, far_x)):
            to_partner(src_x, q, which, 1 - core).wait_recv()

    resident_keys()
    for step in range(CHUNKS + 3):
        if step < 8:
            resident_block(step)
        if step < CHUNKS:
            stage_own(order[step])
        if 1 <= step < CHUNKS + 1:
            stage_near(order[step - 1])
        if 2 <= step < CHUNKS + 2:
            stage_far(order[step - 2])
        if 3 <= step:
            stage_done(order[step - 3])

    slots = 2 * SLOTS
    tail = pages_in[:, :, 0, :, :, 512:WIDE].reshape(slots * 16, 128)
    heads_of = jnp.where(iota((slots, slots * 16), 1) == iota((slots, slots * 16), 0) * 16, 1.0, 0.0)
    marks = dot(heads_of.astype(BF16), tail)
    k_of = iota((slots, 128), 0)
    marks = jnp.where(iota((slots, 128), 1) == 64 + k_of % 4, marks, -BIG)
    present = jnp.where(jnp.max(marks, axis=1, keepdims=True) > -1.0, 1.0, 0.0)

    def owner_of(k):
        dz, dy = slot_offset(k % SLOTS, k // SLOTS)
        return ((z + NZ - dz) % NZ) * NY + (y + 2 * NY - dy) % NY

    eye = iota((slots, slots), 0) == iota((slots, slots), 1)
    present_row = dot(jnp.ones((slots, slots), BF16), jnp.where(eye, present, 0.0).astype(BF16))
    before = owner_of(iota((slots, slots), 1)) < owner_of(iota((slots, slots), 0))
    rank = jnp.sum(jnp.where(before, present_row, 0.0), axis=1, keepdims=True)
    arrivals = jnp.sum(present_row[0:8, :], axis=1, keepdims=True)[0:1, :]
    rank = jnp.where(present > 0.5, rank, -1.0)
    slot_rows = slots * 8
    widen = jnp.where(iota((slot_rows, slots), 0) // 8 == iota((slot_rows, slots), 1), 1.0, 0.0)
    rank_col = dot(widen.astype(BF16), jnp.broadcast_to(rank, (slots, 128)).astype(BF16))[:, 0:1]
    head_col = (iota((slot_rows, 1), 0) % 8).astype(F32)
    goal_col = jnp.where(rank_col > -0.5, rank_col * 8.0 + head_col, -1.0).astype(I32)
    to_slots = jnp.where(goal_col == iota((slot_rows, 512), 1), 1.0, 0.0).astype(BF16)
    narrow = jnp.where(iota((slots, slot_rows), 1) // 8 == iota((slots, slot_rows), 0), rank, 0.0)
    rank_row = dot(jnp.ones((8, slots), BF16), narrow.astype(BF16))[0:1, :]
    head_row = (iota((1, slot_rows), 1) % 8).astype(F32)
    goal_row = jnp.where(rank_row > -0.5, rank_row * 8.0 + head_row, -1.0).astype(I32)
    to_rows = jnp.where(goal_row == iota((512, slot_rows), 0), 1.0, 0.0).astype(BF16)
    fresh_pick = jnp.where(rank.astype(I32) == iota((slots, 64), 1), 1.0, 0.0).astype(BF16)
    slot_fresh[:, 512:WIDE] = jnp.zeros((2 * slots, 128), BF16)
    for j in range(2):
        slot_fresh[j * slots : (j + 1) * slots, 0:LAT] = dot(
            fresh_pick, fresh[j * 64 : j * 64 + 64, :]
        ).astype(BF16)
    for s in range(2):
        at = slice(s * slot_rows, (s + 1) * slot_rows)
        got = dot(to_slots, wide_q[s * 512 : s * 512 + 512, :])
        slot_q[at, 0:512] = got[:, 0:512].astype(BF16)
        lane = iota((slot_rows, 128), 1)
        mark = jnp.where(lane - 64 == (iota((slot_rows, 128), 0) // 8) % 4, 1.0, 0.0)
        slot_q[at, 512:WIDE] = jnp.where(lane < 64, got[:, 512:WIDE], mark).astype(BF16)

    def arrived_block(block):
        page_keys = pages_in[block // CHUNKS, block % CHUNKS].reshape(256, WIDE)
        query = jnp.concatenate(
            [
                slot_q[block * 32 : block * 32 + 32, :],
                slot_q[slot_rows + block * 32 : slot_rows + block * 32 + 32, :],
            ],
            axis=0,
        )
        scores = dot_t(query, page_keys)
        fresh_scores = dot_t(query, slot_fresh[...])
        row = iota((64, 2 * slots), 0)
        lane = iota((64, 2 * slots), 1)
        step = row // 32
        slot = block * 4 + (row % 32) // 8
        fresh_ok = (lane % slots == slot) & (lane // slots <= step)
        fresh_scores = jnp.where(fresh_ok, fresh_scores, -BIG)
        mixed = softmax_mix(scores, fresh_scores, page_keys[:, 0:512], slot_fresh[:, 0:512])
        slot_lat[block * 32 : block * 32 + 32, :] = mixed[0:32]
        slot_lat[slot_rows + block * 32 : slot_rows + block * 32 + 32, :] = mixed[32:64]

    for block in range(2 * CHUNKS):
        arrived_block(block)

    resident_row = (iota((512, 1), 0) // 8).astype(F32) >= arrivals
    for s in range(2):
        rows_at = slice(s * 512, s * 512 + 512)
        moved = dot(to_rows, slot_lat[s * slot_rows : (s + 1) * slot_rows, :])
        for tile in range(4):
            part = moved[:, tile * 128 : tile * 128 + 128]
            lat[tile, rows_at, :] = jnp.where(resident_row, lat[tile, rows_at, :], part)
    for h in range(8):
        per_head = jnp.concatenate(
            [lat[tile, pl.ds(h, 128, stride=8), :].astype(BF16) for tile in range(4)], axis=1
        )
        out[:, h * 128 : h * 128 + 128] = dot(per_head, projection[h]).astype(BF16)

    key_copies = [
        (hop(x, whole, q, right_sems, right), hop(x, whole, q, left_sems, left),
         hop(left_x, first, q, far_right, right), hop(right_x, second, q, far_left, left))
        for q in range(CHUNKS)
    ]
    for q in range(CHUNKS):
        for copy in key_copies[q]:
            copy.wait_send()
        for which, src_x in enumerate((x, left_x, right_x, far_x)):
            to_partner(src_x, q, which, core).wait_send()
    pl.when(core == 1)(lambda: a_copy(0).wait_send())
    for m in range(1, SLOTS):
        a_copy(m).wait_send()


def shards(
    prefill_codes, prefill_scales, page_lists, req_lengths, destinations, pool_codes, pool_scales,
    res_tables, res_lengths, queries, new_latents, value_projection,
):
    slots = 2 * SLOTS
    dma = pltpu.SemaphoreType.DMA
    result = pl.pallas_call(
        kernel,
        out_shape=jax.ShapeDtypeStruct((128, 1024), BF16),
        in_specs=[pl.BlockSpec(memory_space=pltpu.VMEM)] * 12,
        out_specs=pl.BlockSpec(memory_space=pltpu.VMEM),
        scratch_shapes=[
            pltpu.VMEM((2, 256, WIDE), BF16),
            pltpu.VMEM((SLOTS, 16, WIDE), BF16),
            pltpu.VMEM((2, CHUNKS, NX, 4, 16, WIDE), BF16),
            pltpu.VMEM((1152, WIDE), BF16),
            pltpu.VMEM((1024, WIDE), BF16),
            pltpu.VMEM((2 * slots * 8, WIDE), BF16),
            pltpu.VMEM((2 * slots, WIDE), BF16),
            pltpu.VMEM((2 * slots * 8, 512), BF16),
            pltpu.VMEM((4, 1024, 128), F32),
            dma, dma, dma((SLOTS,)), dma((SLOTS,)),
            dma((CHUNKS,)), dma((CHUNKS,)), dma((CHUNKS,)), dma((CHUNKS,)),
            dma((CHUNKS,)), dma((CHUNKS,)), dma((CHUNKS,)), dma((CHUNKS,)),
            dma((CHUNKS, 4)), dma((CHUNKS, 4)), dma,
        ],
        compiler_params=pltpu.CompilerParams(
            collective_id=0, has_side_effects=True, vmem_limit_bytes=48 * 1024 * 1024
        ),
    )(
        prefill_codes.reshape(256, LAT),
        prefill_scales.reshape(256, 4),
        page_lists.reshape(1, 32),
        req_lengths.reshape(1, 32),
        destinations.reshape(1, 32),
        pool_codes.reshape(1024, LAT),
        pool_scales.reshape(1024, 4),
        res_tables,
        res_lengths.reshape(64, 1),
        queries.reshape(1024, LAT),
        new_latents.reshape(128, LAT),
        value_projection,
    )
    return result.reshape(2, 64, 1024)


def solution(mesh):
    return jax.shard_map(
        shards,
        mesh=mesh,
        in_specs=(
            P("inst", "head", None),
            P("inst", "head", None),
            P("inst", None),
            P("inst"),
            P("inst"),
            P("inst", None, None),
            P("inst", None, None),
            P("inst", None),
            P("inst"),
            P(None, "inst", "head", None),
            P(None, "inst", None),
            P("head", None, None),
        ),
        out_specs=P(None, "inst", "head"),
        check_vma=False,
    )
```

time: 157 us -> 86.5 us (0.55)
  the two profiles are of different devices: /device:TPU:1 before, /device:TPU:33 now
where the time goes in v2:
time: 86.5 us; the launch traced here: 86 us
  Pallas kernels  74.3 us (86%)
  local copies, waits for them, and re-layouts  11.7 us (14%)
    pallas_call x1, Pallas kernels, shards(): pl.pallas_call(kernel, out_shape=jax.ShapeDtypeStruct((128, 1024), BF16),...  74.3 us
    unnamed x20, local copies, waits for them, and re-layouts  11 us

profile of v2, /device:TPU:33, one launch (start us, length us, event | category | flops | bytes accessed | tf_op | source)
XLA Modules:
  0.0 86.0 jit_solution(16984254394862709279)
XLA Ops:
  0.0 0.8 copy.15.tables
  0.8 0.7 copy.16.res_lengths
  1.5 0.8 copy.13
  2.4 0.9 %copy.14 = bf16[16,64,4]{2,1,0:T(8,128)(2,1)S(1)} copy(bf16[16,64,4]{1,2,0:T(4,128)(2,1)} %param.18) | data formatting | bytes 16384 | tf_op args[6]
  3.3 0.0 copy-start
  3.3 1.3 %copy-done = bf16[16,64,576]{2,1,0:T(8,128)(2,1)S(1)} copy-done((bf16[16,64,576]{2,1,0:T(8,128)(2,1)S(1)}, bf16[16,64,576]{2,1,0:T(8,128)(2,1)}, u32[]{:S(2)}) %copy-start) | copy-done | bytes 1179672
  4.6 0.0 copy-start.1
  4.6 1.3 %copy-done.1 = bf16[2,64,8,576]{3,2,1,0:T(8,128)(2,1)S(1)} copy-done((bf16[2,64,8,576]{3,2,1,0:T(8,128)(2,1)S(1)}, bf16[2,64,8,576]{3,2,1,0:T(8,128)(2,1)}, u32[]{:S(2)}) %copy-start.1) | copy-done | bytes 1179672
  5.9 0.0 copy-start.2
  5.9 1.2 %copy-done.2 = bf16[8,512,128]{2,1,0:T(8,128)(2,1)S(1)} copy-done((bf16[8,512,128]{2,1,0:T(8,128)(2,1)S(1)}, bf16[8,512,128]{2,1,0:T(8,128)(2,1)}, u32[]{:S(2)}) %copy-start.2) | copy-done | bytes 1048600
  7.2 0.0 copy-start.3
  7.2 1.0 %copy-done.3 = bf16[32,8,576]{2,1,0:T(8,128)(2,1)S(1)} copy-done((bf16[32,8,576]{2,1,0:T(8,128)(2,1)S(1)}, bf16[32,8,576]{2,1,0:T(8,128)(2,1)}, u32[]{:S(2)}) %copy-start.3) | copy-done | bytes 294936
  8.1 0.0 copy-start.4
  8.1 0.9 %copy-done.4 = bf16[2,64,576]{2,1,0:T(8,128)(2,1)S(1)} copy-done((bf16[2,64,576]{2,1,0:T(8,128)(2,1)S(1)}, bf16[2,64,576]{2,1,0:T(8,128)(2,1)}, u32[]{:S(2)}) %copy-start.4) | copy-done | bytes 147480
  9.1 0.0 copy-start.5
  9.1 0.7 copy-done.5
  9.7 0.0 copy-start.6
  9.7 0.7 copy-done.6
  10.4 0.0 copy-start.7
  10.4 0.7 copy-done.7
  11.0 74.3 %shard_map.118 = bf16[128,1024]{1,0:T(8,128)(2,1)S(1)} custom-call(bf16[256,576]{1,0:T(8,128)(2,1)S(1)} %bitcast.15, bf16[256,4]{1,0:T(8,128)(2,1)S(1)} %bitcast.16, s32[1,32]{1,0:T(1,128)S(1)} %bitcast.18, s32[1,32]{1,0:T(1,128)S(1)} %bitcast.19, s32[1,32]{1,0:T(1,128)S(1)} %bitcast.20, bf16[1024,576]{1,0:T(8,128)(2,1)S(1)} %bitcast.11, ...), custom_call_target="tpu_custom_call" | custom-call | tf_op jit(solution)/shard_map/pallas_call | solution.py:341
  85.3 0.7 copy.18
Async XLA Ops:
  3.3 1.3 %copy-start = (bf16[16,64,576]{2,1,0:T(8,128)(2,1)S(1)}, bf16[16,64,576]{2,1,0:T(8,128)(2,1)}, u32[]{:S(2)}) copy-start(bf16[16,64,576]{2,1,0:T(8,128)(2,1)} %param.17) | copy-start | bytes 3538948
  4.6 1.3 %copy-start.1 = (bf16[2,64,8,576]{3,2,1,0:T(8,128)(2,1)S(1)}, bf16[2,64,8,576]{3,2,1,0:T(8,128)(2,1)}, u32[]{:S(2)}) copy-start(bf16[2,64,8,576]{3,2,1,0:T(8,128)(2,1)} %param.21) | copy-start | bytes 3538948
  5.9 1.2 %copy-start.2 = (bf16[8,512,128]{2,1,0:T(8,128)(2,1)S(1)}, bf16[8,512,128]{2,1,0:T(8,128)(2,1)}, u32[]{:S(2)}) copy-start(bf16[8,512,128]{2,1,0:T(8,128)(2,1)} %projection.1) | copy-start | bytes 3145732
  7.2 1.0 %copy-start.3 = (bf16[32,8,576]{2,1,0:T(8,128)(2,1)S(1)}, bf16[32,8,576]{2,1,0:T(8,128)(2,1)}, u32[]{:S(2)}) copy-start(bf16[32,8,576]{2,1,0:T(8,128)(2,1)} %param.12) | copy-start | bytes 884740
  8.1 0.9 %copy-start.4 = (bf16[2,64,576]{2,1,0:T(8,128)(2,1)S(1)}, bf16[2,64,576]{2,1,0:T(8,128)(2,1)}, u32[]{:S(2)}) copy-start(bf16[2,64,576]{2,1,0:T(8,128)(2,1)} %param.22) | copy-start | bytes 442372
  9.1 0.7 copy-start.5
  9.7 0.7 copy-start.6
  10.4 0.7 copy-start.7

commit v3 on v2

--- a/solution.py
+++ b/solution.py
@@ -13,7 +13,9 @@
 WIDE = 640
 NZ, NY, NX = 16, 4, 4
 SLOTS = NZ * NY // 2
-CHUNKS = SLOTS // 4
+BLOCKS = 2 * SLOTS // 4
+GROUPS = ((0, 6), (6, 10), (10, 14), (14, 18), (18, 22), (22, 26), (26, 30), (30, 32))
+LAST = len(GROUPS) - 1
 BIG = 1e30
 MESH = pl.DeviceIdType.MESH
 softmax_scale = (0.1 * math.log(40.0) + 1.0) ** 2 / math.sqrt(192.0)
@@ -33,21 +35,19 @@
 
 
 def slot_offset(m, core):
-    q, sign, half = m // 4, (m // 2) % 2, m % 2
+    pair = m // 2
     if isinstance(m, int):
-        dz = q if sign == 0 else (NZ - q if q else NZ // 2)
+        dz = (pair + 1) // 2 if pair % 2 else (NZ - pair // 2) % NZ
     else:
-        dz = jnp.where(sign == 0, q, jnp.where(q == 0, NZ // 2, NZ - q))
-    return dz, 2 * half + core
-
-
-def dequantize_into(dst, codes, scales, rows, start):
-    for tile in range(4):
-        lanes = slice(tile * 128, tile * 128 + 128)
-        dst[start : start + rows, lanes] = (
-            codes[:, lanes].astype(F32) * scales[:, tile : tile + 1].astype(F32)
-        ).astype(BF16)
-    dst[start : start + rows, 512:LAT] = codes[:, 512:LAT]
+        dz = jnp.where(pair % 2 == 1, (pair + 1) // 2, (NZ - pair // 2) % NZ)
+    return dz, 2 * (m % 2) + core
+
+
+def spread_scales(scales):
+    n = scales.shape[1]
+    scales = scales.astype(F32)
+    spread = [jnp.broadcast_to(scales[j : j + 1, :], (128, n)) for j in range(4)]
+    return jnp.concatenate(spread, axis=0).astype(BF16)
 
 
 def softmax_mix(scores, fresh_scores, values, fresh_values):
@@ -64,17 +64,33 @@
 
 
 def kernel(
-    codes, scales, pages, lengths, dests, pool_codes, pool_scales, tables, res_lengths,
-    queries, fresh, projection, out,
+    codes_hbm, scales_hbm, pages_hbm, lengths_hbm, dests_hbm, pool_codes_hbm, pool_scales_hbm,
+    tables_hbm, res_lengths_hbm, queries_hbm, fresh_hbm, projection_hbm, out,
+    codes, scales, pages, lengths, dests, pool_codes, pool_scales,
+    tables, res_lengths, queries, fresh, projection,
     keys, packed, pages_in, res_keys, wide_q, slot_q, slot_fresh, slot_lat, lat,
-    key_send, key_recv, a_send, a_recv, r_send, r_recv, l_send, l_recv,
+    in_sems, key_send, key_recv, a_send, a_recv, r_send, r_recv, l_send, l_recv,
     rr_send, rr_recv, ll_send, ll_recv, p_send, p_recv, own_sem,
 ):
+    sources = (
+        codes_hbm, scales_hbm, pages_hbm, lengths_hbm, dests_hbm, pool_codes_hbm, pool_scales_hbm,
+        tables_hbm, res_lengths_hbm, queries_hbm, fresh_hbm, projection_hbm,
+    )
+    places = (
+        codes, scales, pages, lengths, dests, pool_codes, pool_scales,
+        tables, res_lengths, queries, fresh, projection,
+    )
+    fetches = [
+        pltpu.make_async_copy(src, dst, in_sems.at[i])
+        for i, (src, dst) in enumerate(zip(sources, places))
+    ]
+    for i in range(5):
+        fetches[i].start()
     inst, head = lax.axis_index("inst"), lax.axis_index("head")
     z, y = inst // NY, inst % NY
     x, core = head // 2, head % 2
     right_x, left_x, far_x = (x + 1) % NX, (x + NX - 1) % NX, (x + 2) % NX
-    right, left = (inst, right_x * 2 + core), (inst, left_x * 2 + core)
+    right, left, far = (inst, right_x * 2 + core), (inst, left_x * 2 + core), (inst, far_x * 2 + core)
     partner = (inst, x * 2 + 1 - core)
 
     def target(m):
@@ -82,7 +98,7 @@
         return (((z + dz) % NZ) * NY + (y + dy) % NY, head)
 
     barrier = pltpu.get_barrier_semaphore()
-    for device in (partner, right, left):
+    for device in (partner, right, left, far):
         pl.semaphore_signal(barrier, inc=1, device_id=device, device_id_type=MESH)
     for m in range(SLOTS):
         if m == 0:
@@ -92,11 +108,25 @@
         else:
             pl.semaphore_signal(barrier, inc=1, device_id=target(m), device_id_type=MESH)
 
+    for i in range(5, len(fetches)):
+        fetches[i].start()
+
     own = keys.at[core]
     own[:, 512:WIDE] = jnp.zeros((256, 128), BF16)
-    dequantize_into(own, codes, scales, 256, 0)
-
-    pl.semaphore_wait(barrier, SLOTS + 2 + core)
+    fetches[0].wait()
+    fetches[1].wait()
+    token_row = iota((256, 32), 0)
+    of_page = token_row // 8 == iota((256, 32), 1)
+    scale_map = jnp.zeros((256, 512), F32)
+    for t in range(8):
+        at_token = jnp.where(of_page & (token_row % 8 == t), 1.0, 0.0).astype(BF16)
+        scale_map = scale_map + dot_t(at_token, spread_scales(scales[t]))
+    own[:, 0:512] = (codes[:, 0:512].astype(F32) * scale_map).astype(BF16)
+    own[:, 512:LAT] = codes[:, 512:LAT]
+    for i in range(2, 5):
+        fetches[i].wait()
+
+    pl.semaphore_wait(barrier, SLOTS + 3 + core)
     key_copy = pltpu.make_async_remote_copy(
         src_ref=own, dst_ref=own, send_sem=key_send, recv_sem=key_recv,
         device_id=partner, device_id_type=MESH,
@@ -130,33 +160,39 @@
 
     def a_copy(m):
         return pltpu.make_async_remote_copy(
-            src_ref=packed.at[m], dst_ref=pages_in.at[core, m // 4, x, m % 4],
+            src_ref=packed.at[m], dst_ref=pages_in.at[core, x, m],
             send_sem=a_send.at[m], recv_sem=a_recv.at[m],
             device_id=target(m), device_id_type=MESH,
         )
 
-    own_copy = pltpu.make_async_copy(packed.at[0], pages_in.at[core, 0, x, 0], own_sem)
-    order = list(range(1, CHUNKS)) + [0]
-    for q in order:
-        for m in range(4 * q, 4 * q + 4):
-            if m == 0:
-                pl.when(core == 1)(lambda: a_copy(0).start())
-                pl.when(core == 0)(lambda: own_copy.start())
-            else:
-                a_copy(m).start()
+    own_copy = pltpu.make_async_copy(packed.at[0], pages_in.at[core, x, 0], own_sem)
+    pl.when(core == 1)(lambda: a_copy(0).start())
+    pl.when(core == 0)(lambda: own_copy.start())
+    for m in range(1, SLOTS):
+        a_copy(m).start()
 
     def resident_keys():
-        listed = jnp.zeros((128, 16), F32)
-        page_ids = iota((64, 16), 1)
+        for i in range(5, len(fetches)):
+            fetches[i].wait()
+        held = jnp.zeros((16, 64), F32)
+        page_ids = iota((16, 64), 0)
         for j in range(8):
             left_over = jnp.clip(res_lengths[...].astype(F32) - 64.0 * j, 0.0, 64.0)
-            part = jnp.where(tables[:, j : j + 1] == page_ids, left_over, 0.0)
-            listed = listed + jnp.concatenate([part, part], axis=0)
+            held = held + jnp.where(tables[j : j + 1, :] == page_ids, left_over, 0.0)
+        shift = jnp.where(iota((64, 128), 0) == iota((64, 128), 1) - 64, 1.0, 0.0).astype(BF16)
+        held = dot(held.astype(BF16), shift).astype(BF16)
         spread = jnp.where(iota((1024, 16), 0) // 64 == iota((1024, 16), 1), 1.0, 0.0).astype(BF16)
-        held = dot_t(spread, listed.astype(BF16))
+        held = dot(spread, held)
         place = (iota((1024, 128), 0) % 64).astype(F32)
-        res_keys[0:1024, 512:WIDE] = jnp.where(place < held, 0.0, -BIG).astype(BF16)
-        dequantize_into(res_keys, pool_codes, pool_scales, 1024, 0)
+        lane = iota((1024, 128), 1)
+        bias = jnp.where((place < held) | (lane < 64), 0.0, -BIG)
+        res_keys[0:1024, 512:WIDE] = bias.astype(BF16)
+        res_keys[0:1024, 512:LAT] = pool_codes[:, 512:LAT]
+        eye = jnp.where(iota((64, 64), 0) == iota((64, 64), 1), 1.0, 0.0).astype(BF16)
+        for p in range(16):
+            at = slice(p * 64, p * 64 + 64)
+            scale_map = dot_t(eye, spread_scales(pool_scales[p]))
+            res_keys[at, 0:512] = (pool_codes[at, 0:512].astype(F32) * scale_map).astype(BF16)
         same = iota((128, 128), 0) % 64 == iota((128, 128), 1) - 64
         res_keys[1024:1152, 512:WIDE] = jnp.where(same, 0.0, -BIG).astype(BF16)
         res_keys[1024:1152, 0:LAT] = fresh[...]
@@ -177,47 +213,67 @@
         for tile in range(4):
             lat[tile, rows_at, :] = mixed[:, tile * 128 : tile * 128 + 128]
 
-    def hop(src_x, piece, q, sems, device):
+    def hop(src_x, span, q, sems, device):
         send, recv = sems
-        ref = pages_in.at[core, q, src_x, piece]
+        ref = pages_in.at[core, src_x, pl.ds(span[0], span[1] - span[0])]
         return pltpu.make_async_remote_copy(
             src_ref=ref, dst_ref=ref, send_sem=send.at[q], recv_sem=recv.at[q],
             device_id=device, device_id_type=MESH,
         )
 
     def to_partner(src_x, q, which, from_core):
-        ref = pages_in.at[from_core, q, src_x]
+        span = GROUPS[q]
+        ref = pages_in.at[from_core, src_x, pl.ds(span[0], span[1] - span[0])]
         return pltpu.make_async_remote_copy(
             src_ref=ref, dst_ref=ref, send_sem=p_send.at[q, which], recv_sem=p_recv.at[q, which],
             device_id=partner, device_id_type=MESH,
         )
 
-    whole, first, second = pl.ds(0, 4), pl.ds(0, 2), pl.ds(2, 2)
     right_sems, left_sems = (r_send, r_recv), (l_send, l_recv)
     far_right, far_left = (rr_send, rr_recv), (ll_send, ll_recv)
 
+    def halves(q):
+        first, last = GROUPS[q]
+        return (first, (first + last) // 2), ((first + last) // 2, last)
+
+    def sent(q):
+        yield hop(x, GROUPS[q], q, right_sems, right)
+        yield hop(x, GROUPS[q], q, left_sems, left)
+        if q == LAST:
+            yield hop(x, GROUPS[q], q, far_right, far)
+        else:
+            yield hop(left_x, halves(q)[0], q, far_right, right)
+            yield hop(right_x, halves(q)[1], q, far_left, left)
+
     def stage_own(q):
-        for m in range(4 * q, 4 * q + 4):
+        for m in range(*GROUPS[q]):
             if m == 0:
                 pl.when(core == 1)(lambda: a_copy(0).wait_recv())
                 pl.when(core == 0)(lambda: own_copy.wait())
             else:
                 a_copy(m).wait_recv()
-        hop(x, whole, q, right_sems, right).start()
-        hop(x, whole, q, left_sems, left).start()
+        hop(x, GROUPS[q], q, right_sems, right).start()
+        hop(x, GROUPS[q], q, left_sems, left).start()
+        if q == LAST:
+            hop(x, GROUPS[q], q, far_right, far).start()
         to_partner(x, q, 0, core).start()
 
     def stage_near(q):
-        hop(left_x, whole, q, right_sems, right).wait_recv()
-        hop(left_x, first, q, far_right, right).start()
+        hop(left_x, GROUPS[q], q, right_sems, right).wait_recv()
+        if q != LAST:
+            hop(left_x, halves(q)[0], q, far_right, right).start()
         to_partner(left_x, q, 1, core).start()
-        hop(right_x, whole, q, left_sems, left).wait_recv()
-        hop(right_x, second, q, far_left, left).start()
+        hop(right_x, GROUPS[q], q, left_sems, left).wait_recv()
+        if q != LAST:
+            hop(right_x, halves(q)[1], q, far_left, left).start()
         to_partner(right_x, q, 2, core).start()
 
     def stage_far(q):
-        hop(far_x, first, q, far_right, right).wait_recv()
-        hop(far_x, second, q, far_left, left).wait_recv()
+        if q == LAST:
+            hop(far_x, GROUPS[q], q, far_right, far).wait_recv()
+        else:
+            hop(far_x, halves(q)[0], q, far_right, right).wait_recv()
+            hop(far_x, halves(q)[1], q, far_left, left).wait_recv()
         to_partner(far_x, q, 3, core).start()
 
     def stage_done(q):
@@ -225,20 +281,21 @@
             to_partner(src_x, q, which, 1 - core).wait_recv()
 
     resident_keys()
-    for step in range(CHUNKS + 3):
+    steps = len(GROUPS)
+    for step in range(steps + 3):
         if step < 8:
             resident_block(step)
-        if step < CHUNKS:
-            stage_own(order[step])
-        if 1 <= step < CHUNKS + 1:
-            stage_near(order[step - 1])
-        if 2 <= step < CHUNKS + 2:
-            stage_far(order[step - 2])
+        if step < steps:
+            stage_own(step)
+        if 1 <= step < steps + 1:
+            stage_near(step - 1)
+        if 2 <= step < steps + 2:
+            stage_far(step - 2)
         if 3 <= step:
-            stage_done(order[step - 3])
+            stage_done(step - 3)
 
     slots = 2 * SLOTS
-    tail = pages_in[:, :, 0, :, :, 512:WIDE].reshape(slots * 16, 128)
+    tail = pages_in[:, 0, :, :, 512:WIDE].reshape(slots * 16, 128)
     heads_of = jnp.where(iota((slots, slots * 16), 1) == iota((slots, slots * 16), 0) * 16, 1.0, 0.0)
     marks = dot(heads_of.astype(BF16), tail)
     k_of = iota((slots, 128), 0)
@@ -281,7 +338,8 @@
         slot_q[at, 512:WIDE] = jnp.where(lane < 64, got[:, 512:WIDE], mark).astype(BF16)
 
     def arrived_block(block):
-        page_keys = pages_in[block // CHUNKS, block % CHUNKS].reshape(256, WIDE)
+        slot = block % (BLOCKS // 2) * 4
+        page_keys = pages_in[block // (BLOCKS // 2), :, slot : slot + 4].reshape(256, WIDE)
         query = jnp.concatenate(
             [
                 slot_q[block * 32 : block * 32 + 32, :],
@@ -301,7 +359,7 @@
         slot_lat[block * 32 : block * 32 + 32, :] = mixed[0:32]
         slot_lat[slot_rows + block * 32 : slot_rows + block * 32 + 32, :] = mixed[32:64]
 
-    for block in range(2 * CHUNKS):
+    for block in range(BLOCKS):
         arrived_block(block)
 
     resident_row = (iota((512, 1), 0) // 8).astype(F32) >= arrivals
@@ -317,13 +375,8 @@
         )
         out[:, h * 128 : h * 128 + 128] = dot(per_head, projection[h]).astype(BF16)
 
-    key_copies = [
-        (hop(x, whole, q, right_sems, right), hop(x, whole, q, left_sems, left),
-         hop(left_x, first, q, far_right, right), hop(right_x, second, q, far_left, left))
-        for q in range(CHUNKS)
-    ]
-    for q in range(CHUNKS):
-        for copy in key_copies[q]:
+    for q in range(steps):
+        for copy in sent(q):
             copy.wait_send()
         for which, src_x in enumerate((x, left_x, right_x, far_x)):
             to_partner(src_x, q, which, core).wait_send()
@@ -338,43 +391,45 @@
 ):
     slots = 2 * SLOTS
     dma = pltpu.SemaphoreType.DMA
+    operands = (
+        prefill_codes.reshape(256, LAT),
+        jnp.transpose(prefill_scales, (1, 2, 0)),
+        page_lists.reshape(1, 32),
+        req_lengths.reshape(1, 32),
+        destinations.reshape(1, 32),
+        pool_codes.reshape(1024, LAT),
+        jnp.transpose(pool_scales, (0, 2, 1)),
+        jnp.transpose(res_tables),
+        res_lengths.reshape(1, 64),
+        queries.reshape(1024, LAT),
+        new_latents.reshape(128, LAT),
+        value_projection,
+    )
+    groups = dma((len(GROUPS),))
     result = pl.pallas_call(
         kernel,
         out_shape=jax.ShapeDtypeStruct((128, 1024), BF16),
-        in_specs=[pl.BlockSpec(memory_space=pltpu.VMEM)] * 12,
+        in_specs=[pl.BlockSpec(memory_space=pltpu.HBM)] * 12,
         out_specs=pl.BlockSpec(memory_space=pltpu.VMEM),
-        scratch_shapes=[
+        scratch_shapes=[pltpu.VMEM(item.shape, item.dtype) for item in operands]
+        + [
             pltpu.VMEM((2, 256, WIDE), BF16),
             pltpu.VMEM((SLOTS, 16, WIDE), BF16),
-            pltpu.VMEM((2, CHUNKS, NX, 4, 16, WIDE), BF16),
+            pltpu.VMEM((2, NX, SLOTS, 16, WIDE), BF16),
             pltpu.VMEM((1152, WIDE), BF16),
             pltpu.VMEM((1024, WIDE), BF16),
             pltpu.VMEM((2 * slots * 8, WIDE), BF16),
             pltpu.VMEM((2 * slots, WIDE), BF16),
             pltpu.VMEM((2 * slots * 8, 512), BF16),
             pltpu.VMEM((4, 1024, 128), F32),
-            dma, dma, dma((SLOTS,)), dma((SLOTS,)),
-            dma((CHUNKS,)), dma((CHUNKS,)), dma((CHUNKS,)), dma((CHUNKS,)),
-            dma((CHUNKS,)), dma((CHUNKS,)), dma((CHUNKS,)), dma((CHUNKS,)),
-            dma((CHUNKS, 4)), dma((CHUNKS, 4)), dma,
+            dma((12,)), dma, dma, dma((SLOTS,)), dma((SLOTS,)),
+            groups, groups, groups, groups, groups, groups, groups, groups,
+            dma((len(GROUPS), 4)), dma((len(GROUPS), 4)), dma,
         ],
         compiler_params=pltpu.CompilerParams(
-            collective_id=0, has_side_effects=True, vmem_limit_bytes=48 * 1024 * 1024
+            collective_id=0, has_side_effects=True, vmem_limit_bytes=64 * 1024 * 1024
         ),
-    )(
-        prefill_codes.reshape(256, LAT),
-        prefill_scales.reshape(256, 4),
-        page_lists.reshape(1, 32),
-        req_lengths.reshape(1, 32),
-        destinations.reshape(1, 32),
-        pool_codes.reshape(1024, LAT),
-        pool_scales.reshape(1024, 4),
-        res_tables,
-        res_lengths.reshape(64, 1),
-        queries.reshape(1024, LAT),
-        new_latents.reshape(128, LAT),
-        value_projection,
-    )
+    )(*operands)
     return result.reshape(2, 64, 1024)
 
 

time: 86.5 us -> 75.4 us (0.87)
  local copies, waits for them, and re-layouts: 11.7 us -> 1.67 us
    unnamed x20 -> x1, local copies, waits for them, and re-layouts: 11 us -> 1.67 us
where the time goes in v3:
time: 75.4 us; the launch traced here: 75.2 us
  Pallas kernels  73.6 us (98%)
  local copies, waits for them, and re-layouts  1.67 us (2%)
    pallas_call x1, Pallas kernels, shards(): pl.pallas_call(kernel, out_shape=jax.ShapeDtypeStruct((128, 1024), BF16),...  73.6 us
    unnamed x1, local copies, waits for them, and re-layouts  1.67 us

profile of v3, /device:TPU:33, one launch (start us, length us, event | category | flops | bytes accessed | tf_op | source)
XLA Modules:
  0.0 75.2 jit_solution(8914088292628626703)
XLA Ops:
  0.0 73.6 %shard_map.118 = bf16[128,1024]{1,0:T(8,128)(2,1)} custom-call(bf16[256,576]{1,0:T(8,128)(2,1)} %bitcast.15, bf16[8,4,32]{2,1,0:T(4,128)(2,1)} %bitcast.18, s32[1,32]{1,0:T(1,128)} %bitcast.20, s32[1,32]{1,0:T(1,128)} %bitcast.21, s32[1,32]{1,0:T(1,128)} %bitcast.22, bf16[1024,576]{1,0:T(8,128)(2,1)} %bitcast.12, bf16[16,4,64]{2,1,0:T(4,128)(2,1)} %bitcast.17, ...), custom_call_target="tpu_custom_call" | custom-call | tf_op jit(solution)/shard_map/pallas_call | solution.py:409
  73.6 1.7 %copy.14 = bf16[2,64,1024]{2,1,0:T(8,128)(2,1)} copy(bf16[2,64,1024]{2,1,0:T(8,128)(2,1)} %bitcast.14) | data formatting | bytes 524288

commit v4 on v3

--- a/solution.py
+++ b/solution.py
@@ -69,8 +69,10 @@
     codes, scales, pages, lengths, dests, pool_codes, pool_scales,
     tables, res_lengths, queries, fresh, projection,
     keys, packed, pages_in, res_keys, wide_q, slot_q, slot_fresh, slot_lat, lat,
+    meta, meta_in, slot_out, res_out,
     in_sems, key_send, key_recv, a_send, a_recv, r_send, r_recv, l_send, l_recv,
     rr_send, rr_recv, ll_send, ll_recv, p_send, p_recv, own_sem,
+    m_send, m_recv, g_send, g_recv, meta_sem,
 ):
     sources = (
         codes_hbm, scales_hbm, pages_hbm, lengths_hbm, dests_hbm, pool_codes_hbm, pool_scales_hbm,
@@ -97,6 +99,8 @@
         dz, dy = slot_offset(m, core)
         return (((z + dz) % NZ) * NY + (y + dy) % NY, head)
 
+    target_of = target
+
     barrier = pltpu.get_barrier_semaphore()
     for device in (partner, right, left, far):
         pl.semaphore_signal(barrier, inc=1, device_id=device, device_id_type=MESH)
@@ -139,6 +143,39 @@
     wanted = ((z + dz) % NZ) * NY + (y + dy) % NY
     hit = dests[...] == wanted
     page = jnp.sum(jnp.where(hit, pages[...].astype(F32) + 1.0, 0.0), axis=1, keepdims=True)
+    marks = jnp.broadcast_to(jnp.where(page > 0.5, 1.0, 0.0), (rows, 128))
+    meta[...] = marks.reshape(SLOTS, 2, 8, 128)[:, 0]
+
+    def meta_copy(a):
+        return pltpu.make_async_remote_copy(
+            src_ref=meta.at[4 * a + x], dst_ref=meta_in.at[core, x, a],
+            send_sem=m_send.at[a], recv_sem=m_recv.at[a],
+            device_id=target_of(4 * a + x), device_id_type=MESH,
+        )
+
+    def meta_own():
+        return pltpu.make_async_copy(meta.at[0], meta_in.at[core, x, 0], meta_sem)
+
+    to_self = (core == 0) & (x == 0)
+    pl.when(jnp.logical_not(to_self))(lambda: meta_copy(0).start())
+    pl.when(to_self)(lambda: meta_own().start())
+    for a in range(1, SLOTS // NX):
+        meta_copy(a).start()
+
+    def meta_gather(i):
+        ref = meta_in.at[core, x]
+        return pltpu.make_async_remote_copy(
+            src_ref=ref, dst_ref=ref, send_sem=g_send.at[i], recv_sem=g_recv.at[i],
+            device_id=(right, left, far)[i], device_id_type=MESH,
+        )
+
+    def meta_partner(from_core):
+        ref = meta_in.at[from_core]
+        return pltpu.make_async_remote_copy(
+            src_ref=ref, dst_ref=ref, send_sem=g_send.at[3], recv_sem=g_recv.at[3],
+            device_id=partner, device_id_type=MESH,
+        )
+
     count = jnp.sum(jnp.where(hit, lengths[...].astype(F32), 0.0), axis=1, keepdims=True)
     slot_row = iota((rows, 1), 0)
     token = slot_row % 16
@@ -239,7 +276,7 @@
     def sent(q):
         yield hop(x, GROUPS[q], q, right_sems, right)
         yield hop(x, GROUPS[q], q, left_sems, left)
-        if q == LAST:
+        if True:
             yield hop(x, GROUPS[q], q, far_right, far)
         else:
             yield hop(left_x, halves(q)[0], q, far_right, right)
@@ -254,22 +291,18 @@
                 a_copy(m).wait_recv()
         hop(x, GROUPS[q], q, right_sems, right).start()
         hop(x, GROUPS[q], q, left_sems, left).start()
-        if q == LAST:
+        if True:
             hop(x, GROUPS[q], q, far_right, far).start()
         to_partner(x, q, 0, core).start()
 
     def stage_near(q):
         hop(left_x, GROUPS[q], q, right_sems, right).wait_recv()
-        if q != LAST:
-            hop(left_x, halves(q)[0], q, far_right, right).start()
         to_partner(left_x, q, 1, core).start()
         hop(right_x, GROUPS[q], q, left_sems, left).wait_recv()
-        if q != LAST:
-            hop(right_x, halves(q)[1], q, far_left, left).start()
         to_partner(right_x, q, 2, core).start()
 
     def stage_far(q):
-        if q == LAST:
+        if True:
             hop(far_x, GROUPS[q], q, far_right, far).wait_recv()
         else:
             hop(far_x, halves(q)[0], q, far_right, right).wait_recv()
@@ -279,6 +312,92 @@
     def stage_done(q):
         for which, src_x in enumerate((x, left_x, right_x, far_x)):
             to_partner(src_x, q, which, 1 - core).wait_recv()
+
+    slots = 2 * SLOTS
+
+    def meta_first():
+        pl.when(jnp.logical_not(to_self))(lambda: meta_copy(0).wait_recv())
+        pl.when(to_self)(lambda: meta_own().wait())
+        for a in range(1, SLOTS // NX):
+            meta_copy(a).wait_recv()
+        for i in range(3):
+            meta_gather(i).start()
+
+    def meta_second():
+        for i in range(3):
+            meta_gather(i).wait_recv()
+        meta_partner(core).start()
+
+    def owner_of(k):
+        dz, dy = slot_offset(k % SLOTS, k // SLOTS)
+        return ((z + NZ - dz) % NZ) * NY + (y + 2 * NY - dy) % NY
+
+    def slot_rows_of():
+        meta_partner(1 - core).wait_recv()
+        k = iota((slots, slots * 8), 0)
+        at = ((k // SLOTS) * SLOTS + (k % 4) * (SLOTS // 4) + (k % SLOTS) // 4) * 8
+        pick = jnp.where(iota((slots, slots * 8), 1) == at, 1.0, 0.0).astype(BF16)
+        present = dot(pick, meta_in[...].reshape(slots * 8, 128).astype(BF16))[:, 0:1]
+        eye = iota((slots, slots), 0) == iota((slots, slots), 1)
+        present_row = dot(jnp.ones((slots, slots), BF16), jnp.where(eye, present, 0.0).astype(BF16))
+        before = owner_of(iota((slots, slots), 1)) < owner_of(iota((slots, slots), 0))
+        rank = jnp.sum(jnp.where(before, present_row, 0.0), axis=1, keepdims=True)
+        arrivals = jnp.sum(present_row[0:8, :], axis=1, keepdims=True)[0:1, :]
+        rank = jnp.where(present > 0.5, rank, -1.0)
+        ranks = jnp.broadcast_to(rank, (slots, 128)).astype(BF16)
+        widen = jnp.where(iota((512, slots), 0) // 8 == iota((512, slots), 1), 1.0, 0.0)
+        rank_col = dot(widen.astype(BF16), ranks)[:, 0:1]
+        head_col = (iota((512, 1), 0) % 8).astype(F32)
+        goal_col = jnp.where(rank_col > -0.5, rank_col * 8.0 + head_col, -1.0).astype(I32)
+        to_slots = jnp.where(goal_col == iota((512, 512), 1), 1.0, 0.0).astype(BF16)
+        fresh_pick = jnp.where(rank.astype(I32) == iota((slots, 64), 1), 1.0, 0.0).astype(BF16)
+        slot_fresh[:, 512:WIDE] = jnp.zeros((2 * slots, 128), BF16)
+        for j in range(2):
+            slot_fresh[j * slots : (j + 1) * slots, 0:LAT] = dot(
+                fresh_pick, fresh[j * 64 : j * 64 + 64, :]
+            ).astype(BF16)
+        lane = iota((512, 128), 1)
+        mark = jnp.where(lane - 64 == (iota((512, 128), 0) // 8) % 4, 1.0, 0.0)
+        for s in range(2):
+            got = dot(to_slots, wide_q[s * 512 : s * 512 + 512, :])
+            slot_q[:, s, :, 0:512] = got[:, 0:512].astype(BF16).reshape(BLOCKS, 32, 512)
+            last = jnp.where(lane < 64, got[:, 512:WIDE], mark).astype(BF16)
+            slot_q[:, s, :, 512:WIDE] = last.reshape(BLOCKS, 32, 128)
+        n = iota((slots, 128), 1)
+        spot = jnp.where(n // 8 * 4 + n % 4 == iota((slots, 128), 0), rank, 0.0)
+        rank_row = dot(jnp.ones((8, slots), BF16), spot.astype(BF16))[0:1, :]
+        n = iota((128, 128), 1)
+        row = iota((128, 128), 0)
+        same = (rank_row.astype(I32) == row % 64) & (n // 4 % 2 == row // 64)
+        return jnp.where(same, 1.0, 0.0).astype(BF16), arrivals
+
+    def arrived_blocks(*blocks):
+        queries_of = [slot_q[block].reshape(64, WIDE) for block in blocks]
+        keys_of = []
+        for block in blocks:
+            at = block % (BLOCKS // 2) * 4
+            keys_of.append(pages_in[block // (BLOCKS // 2), :, at : at + 4].reshape(256, WIDE))
+        row, lane = iota((64, 2 * slots), 0), iota((64, 2 * slots), 1)
+        results = []
+        for block, query, page_keys in zip(blocks, queries_of, keys_of):
+            scores = dot_t(query, page_keys)
+            fresh_scores = dot_t(query, slot_fresh[...])
+            slot = block * 4 + (row % 32) // 8
+            fresh_ok = (lane % slots == slot) & (lane // slots <= row // 32)
+            results.append((scores, jnp.where(fresh_ok, fresh_scores, -BIG)))
+        for block, page_keys, (scores, fresh_scores) in zip(blocks, keys_of, results):
+            mixed = softmax_mix(scores, fresh_scores, page_keys[:, 0:512], slot_fresh[:, 0:512])
+            mixed = mixed.astype(F32)
+            for tile in range(4):
+                slot_lat[tile, block * 64 : block * 64 + 64, :] = mixed[:, tile * 128 : tile * 128 + 128]
+
+    def project(source, start, count):
+        results = []
+        for h in range(8):
+            at = pl.ds(start * 8 + h, count, stride=8)
+            per_head = jnp.concatenate([source[t, at, :].astype(BF16) for t in range(4)], axis=1)
+            results.append(dot(per_head, projection[h]).astype(BF16))
+        return jnp.concatenate(results, axis=1)
 
     resident_keys()
     steps = len(GROUPS)
@@ -291,90 +410,36 @@
             stage_near(step - 1)
         if 2 <= step < steps + 2:
             stage_far(step - 2)
+        if step == 0:
+            meta_first()
+        if step == 1:
+            meta_second()
+        if step == 2:
+            to_rows, arrivals = slot_rows_of()
+        if step == 8:
+            res_out[...] = project(lat, 0, 128)
         if 3 <= step:
             stage_done(step - 3)
-
-    slots = 2 * SLOTS
-    tail = pages_in[:, 0, :, :, 512:WIDE].reshape(slots * 16, 128)
-    heads_of = jnp.where(iota((slots, slots * 16), 1) == iota((slots, slots * 16), 0) * 16, 1.0, 0.0)
-    marks = dot(heads_of.astype(BF16), tail)
-    k_of = iota((slots, 128), 0)
-    marks = jnp.where(iota((slots, 128), 1) == 64 + k_of % 4, marks, -BIG)
-    present = jnp.where(jnp.max(marks, axis=1, keepdims=True) > -1.0, 1.0, 0.0)
-
-    def owner_of(k):
-        dz, dy = slot_offset(k % SLOTS, k // SLOTS)
-        return ((z + NZ - dz) % NZ) * NY + (y + 2 * NY - dy) % NY
-
-    eye = iota((slots, slots), 0) == iota((slots, slots), 1)
-    present_row = dot(jnp.ones((slots, slots), BF16), jnp.where(eye, present, 0.0).astype(BF16))
-    before = owner_of(iota((slots, slots), 1)) < owner_of(iota((slots, slots), 0))
-    rank = jnp.sum(jnp.where(before, present_row, 0.0), axis=1, keepdims=True)
-    arrivals = jnp.sum(present_row[0:8, :], axis=1, keepdims=True)[0:1, :]
-    rank = jnp.where(present > 0.5, rank, -1.0)
-    slot_rows = slots * 8
-    widen = jnp.where(iota((slot_rows, slots), 0) // 8 == iota((slot_rows, slots), 1), 1.0, 0.0)
-    rank_col = dot(widen.astype(BF16), jnp.broadcast_to(rank, (slots, 128)).astype(BF16))[:, 0:1]
-    head_col = (iota((slot_rows, 1), 0) % 8).astype(F32)
-    goal_col = jnp.where(rank_col > -0.5, rank_col * 8.0 + head_col, -1.0).astype(I32)
-    to_slots = jnp.where(goal_col == iota((slot_rows, 512), 1), 1.0, 0.0).astype(BF16)
-    narrow = jnp.where(iota((slots, slot_rows), 1) // 8 == iota((slots, slot_rows), 0), rank, 0.0)
-    rank_row = dot(jnp.ones((8, slots), BF16), narrow.astype(BF16))[0:1, :]
-    head_row = (iota((1, slot_rows), 1) % 8).astype(F32)
-    goal_row = jnp.where(rank_row > -0.5, rank_row * 8.0 + head_row, -1.0).astype(I32)
-    to_rows = jnp.where(goal_row == iota((512, slot_rows), 0), 1.0, 0.0).astype(BF16)
-    fresh_pick = jnp.where(rank.astype(I32) == iota((slots, 64), 1), 1.0, 0.0).astype(BF16)
-    slot_fresh[:, 512:WIDE] = jnp.zeros((2 * slots, 128), BF16)
-    for j in range(2):
-        slot_fresh[j * slots : (j + 1) * slots, 0:LAT] = dot(
-            fresh_pick, fresh[j * 64 : j * 64 + 64, :]
-        ).astype(BF16)
-    for s in range(2):
-        at = slice(s * slot_rows, (s + 1) * slot_rows)
-        got = dot(to_slots, wide_q[s * 512 : s * 512 + 512, :])
-        slot_q[at, 0:512] = got[:, 0:512].astype(BF16)
-        lane = iota((slot_rows, 128), 1)
-        mark = jnp.where(lane - 64 == (iota((slot_rows, 128), 0) // 8) % 4, 1.0, 0.0)
-        slot_q[at, 512:WIDE] = jnp.where(lane < 64, got[:, 512:WIDE], mark).astype(BF16)
-
-    def arrived_block(block):
-        slot = block % (BLOCKS // 2) * 4
-        page_keys = pages_in[block // (BLOCKS // 2), :, slot : slot + 4].reshape(256, WIDE)
-        query = jnp.concatenate(
-            [
-                slot_q[block * 32 : block * 32 + 32, :],
-                slot_q[slot_rows + block * 32 : slot_rows + block * 32 + 32, :],
-            ],
-            axis=0,
-        )
-        scores = dot_t(query, page_keys)
-        fresh_scores = dot_t(query, slot_fresh[...])
-        row = iota((64, 2 * slots), 0)
-        lane = iota((64, 2 * slots), 1)
-        step = row // 32
-        slot = block * 4 + (row % 32) // 8
-        fresh_ok = (lane % slots == slot) & (lane // slots <= step)
-        fresh_scores = jnp.where(fresh_ok, fresh_scores, -BIG)
-        mixed = softmax_mix(scores, fresh_scores, page_keys[:, 0:512], slot_fresh[:, 0:512])
-        slot_lat[block * 32 : block * 32 + 32, :] = mixed[0:32]
-        slot_lat[slot_rows + block * 32 : slot_rows + block * 32 + 32, :] = mixed[32:64]
-
-    for block in range(BLOCKS):
-        arrived_block(block)
-
-    resident_row = (iota((512, 1), 0) // 8).astype(F32) >= arrivals
-    for s in range(2):
-        rows_at = slice(s * 512, s * 512 + 512)
-        moved = dot(to_rows, slot_lat[s * slot_rows : (s + 1) * slot_rows, :])
-        for tile in range(4):
-            part = moved[:, tile * 128 : tile * 128 + 128]
-            lat[tile, rows_at, :] = jnp.where(resident_row, lat[tile, rows_at, :], part)
-    for h in range(8):
-        per_head = jnp.concatenate(
-            [lat[tile, pl.ds(h, 128, stride=8), :].astype(BF16) for tile in range(4)], axis=1
-        )
-        out[:, h * 128 : h * 128 + 128] = dot(per_head, projection[h]).astype(BF16)
-
+            block = step - 3
+            arrived_blocks(block, block + BLOCKS // 2)
+            half = BLOCKS // 2
+            if block == half - 2:
+                slot_out[0:56, :] = project(slot_lat, 0, 56)
+                slot_out[64:120, :] = project(slot_lat, 64, 56)
+            if block == half - 1:
+                slot_out[56:64, :] = project(slot_lat, 56, 8)
+                slot_out[120:128, :] = project(slot_lat, 120, 8)
+
+    moved = dot(to_rows, slot_out[...])
+    resident_row = (iota((128, 1), 0) % 64).astype(F32) >= arrivals
+    out[...] = jnp.where(resident_row, res_out[...].astype(F32), moved).astype(BF16)
+
+    pl.when(jnp.logical_not(to_self))(lambda: meta_copy(0).wait_send())
+    for a in range(1, SLOTS // NX):
+        meta_copy(a).wait_send()
+    for i in range(3):
+        meta_gather(i).wait_send()
+    meta_partner(core).wait_send()
     for q in range(steps):
         for copy in sent(q):
             copy.wait_send()
@@ -418,13 +483,18 @@
             pltpu.VMEM((2, NX, SLOTS, 16, WIDE), BF16),
             pltpu.VMEM((1152, WIDE), BF16),
             pltpu.VMEM((1024, WIDE), BF16),
-            pltpu.VMEM((2 * slots * 8, WIDE), BF16),
+            pltpu.VMEM((BLOCKS, 2, 32, WIDE), BF16),
             pltpu.VMEM((2 * slots, WIDE), BF16),
-            pltpu.VMEM((2 * slots * 8, 512), BF16),
+            pltpu.VMEM((4, BLOCKS * 64, 128), F32),
             pltpu.VMEM((4, 1024, 128), F32),
+            pltpu.VMEM((SLOTS, 8, 128), F32),
+            pltpu.VMEM((2, NX, SLOTS // NX, 8, 128), F32),
+            pltpu.VMEM((128, 1024), BF16),
+            pltpu.VMEM((128, 1024), BF16),
             dma((12,)), dma, dma, dma((SLOTS,)), dma((SLOTS,)),
             groups, groups, groups, groups, groups, groups, groups, groups,
             dma((len(GROUPS), 4)), dma((len(GROUPS), 4)), dma,
+            dma((SLOTS // NX,)), dma((SLOTS // NX,)), dma((4,)), dma((4,)), dma,
         ],
         compiler_params=pltpu.CompilerParams(
             collective_id=0, has_side_effects=True, vmem_limit_bytes=64 * 1024 * 1024

time: 75.4 us -> 67.3 us (0.89)
  the two profiles are of different devices: /device:TPU:33 before, /device:TPU:1 now
where the time goes in v4:
time: 67.3 us; the launch traced here: 66.9 us
  Pallas kernels  65.2 us (97%)
  local copies, waits for them, and re-layouts  1.67 us (2%)
    pallas_call x1, Pallas kernels, shards(): pl.pallas_call(kernel, out_shape=jax.ShapeDtypeStruct((128, 1024), BF16),...  65.2 us
    unnamed x1, local copies, waits for them, and re-layouts  1.67 us

profile of v4, /device:TPU:1, one launch (start us, length us, event | category | flops | bytes accessed | tf_op | source)
XLA Modules:
  0.0 66.9 jit_solution(9302183389051186321)
XLA Ops:
  0.0 65.2 %shard_map.118 = bf16[128,1024]{1,0:T(8,128)(2,1)} custom-call(bf16[256,576]{1,0:T(8,128)(2,1)} %bitcast.15, bf16[8,4,32]{2,1,0:T(4,128)(2,1)} %bitcast.18, s32[1,32]{1,0:T(1,128)} %bitcast.20, s32[1,32]{1,0:T(1,128)} %bitcast.21, s32[1,32]{1,0:T(1,128)} %bitcast.22, bf16[1024,576]{1,0:T(8,128)(2,1)} %bitcast.12, bf16[16,4,64]{2,1,0:T(4,128)(2,1)} %bitcast.17, ...), custom_call_target="tpu_custom_call" | custom-call | tf_op jit(solution)/shard_map/pallas_call | solution.py:474
  65.2 1.7 %copy.14 = bf16[2,64,1024]{2,1,0:T(8,128)(2,1)} copy(bf16[2,64,1024]{2,1,0:T(8,128)(2,1)} %bitcast.14) | data formatting | bytes 524288

commit v5 on v4

--- a/solution.py
+++ b/solution.py
@@ -15,7 +15,6 @@
 SLOTS = NZ * NY // 2
 BLOCKS = 2 * SLOTS // 4
 GROUPS = ((0, 6), (6, 10), (10, 14), (14, 18), (18, 22), (22, 26), (26, 30), (30, 32))
-LAST = len(GROUPS) - 1
 BIG = 1e30
 MESH = pl.DeviceIdType.MESH
 softmax_scale = (0.1 * math.log(40.0) + 1.0) ** 2 / math.sqrt(192.0)
@@ -70,8 +69,7 @@
     tables, res_lengths, queries, fresh, projection,
     keys, packed, pages_in, res_keys, wide_q, slot_q, slot_fresh, slot_lat, lat,
     meta, meta_in, slot_out, res_out,
-    in_sems, key_send, key_recv, a_send, a_recv, r_send, r_recv, l_send, l_recv,
-    rr_send, rr_recv, ll_send, ll_recv, p_send, p_recv, own_sem,
+    in_sems, key_send, key_recv, a_send, a_recv, h_send, h_recv, p_send, p_recv,
     m_send, m_recv, g_send, g_recv, meta_sem,
 ):
     sources = (
@@ -187,26 +185,30 @@
     mine = (lane - 64) == (slot_row // 16) % 4
     bias = jnp.where(lane < 68, jnp.where(mine & valid, 0.0, -BIG), 0.0)
 
+    group_of = [q for q, (first, last) in enumerate(GROUPS) for _ in range(first, last)]
+
+    def a_copy(m):
+        return pltpu.make_async_remote_copy(
+            src_ref=packed.at[m], dst_ref=pages_in.at[core, x, m],
+            send_sem=a_send.at[min(m, 1)], recv_sem=a_recv.at[group_of[m]],
+            device_id=target(m), device_id_type=MESH,
+        )
+
+    own_copy = pltpu.make_async_copy(packed.at[0], pages_in.at[core, x, 0], a_recv.at[0])
     key_copy.wait()
     both = keys[...].reshape(512, WIDE)
-    for tile in range(4):
-        lanes = slice(tile * 128, tile * 128 + 128)
-        packed[:, :, lanes] = dot(choose, both[:, lanes]).astype(BF16).reshape(SLOTS, 16, 128)
-    last = dot(choose, both[:, 512:WIDE])
-    packed[:, :, 512:WIDE] = jnp.where(lane < 64, last, bias).astype(BF16).reshape(SLOTS, 16, 128)
-
-    def a_copy(m):
-        return pltpu.make_async_remote_copy(
-            src_ref=packed.at[m], dst_ref=pages_in.at[core, x, m],
-            send_sem=a_send.at[m], recv_sem=a_recv.at[m],
-            device_id=target(m), device_id_type=MESH,
-        )
-
-    own_copy = pltpu.make_async_copy(packed.at[0], pages_in.at[core, x, 0], own_sem)
-    pl.when(core == 1)(lambda: a_copy(0).start())
-    pl.when(core == 0)(lambda: own_copy.start())
-    for m in range(1, SLOTS):
-        a_copy(m).start()
+    for part in range(4):
+        at, to = slice(part * 128, part * 128 + 128), slice(part * 8, part * 8 + 8)
+        got = dot(choose[at], both)
+        packed[to, :, 0:512] = got[:, 0:512].astype(BF16).reshape(8, 16, 512)
+        last = jnp.where(lane[at] < 64, got[:, 512:WIDE], bias[at])
+        packed[to, :, 512:WIDE] = last.astype(BF16).reshape(8, 16, 128)
+        for m in range(part * 8, part * 8 + 8):
+            if m == 0:
+                pl.when(core == 1)(lambda: a_copy(0).start())
+                pl.when(core == 0)(lambda: own_copy.start())
+            else:
+                a_copy(m).start()
 
     def resident_keys():
         for i in range(5, len(fetches)):
@@ -250,68 +252,38 @@
         for tile in range(4):
             lat[tile, rows_at, :] = mixed[:, tile * 128 : tile * 128 + 128]
 
-    def hop(src_x, span, q, sems, device):
-        send, recv = sems
+    def hop(src_x, q, way, device):
+        span = GROUPS[q]
         ref = pages_in.at[core, src_x, pl.ds(span[0], span[1] - span[0])]
         return pltpu.make_async_remote_copy(
-            src_ref=ref, dst_ref=ref, send_sem=send.at[q], recv_sem=recv.at[q],
+            src_ref=ref, dst_ref=ref, send_sem=h_send.at[way], recv_sem=h_recv.at[q, way],
             device_id=device, device_id_type=MESH,
         )
 
-    def to_partner(src_x, q, which, from_core):
+    def to_partner(q, from_core):
         span = GROUPS[q]
-        ref = pages_in.at[from_core, src_x, pl.ds(span[0], span[1] - span[0])]
-        return pltpu.make_async_remote_copy(
-            src_ref=ref, dst_ref=ref, send_sem=p_send.at[q, which], recv_sem=p_recv.at[q, which],
+        ref = pages_in.at[from_core, :, pl.ds(span[0], span[1] - span[0])]
+        return pltpu.make_async_remote_copy(
+            src_ref=ref, dst_ref=ref, send_sem=p_send, recv_sem=p_recv.at[q],
             device_id=partner, device_id_type=MESH,
         )
 
-    right_sems, left_sems = (r_send, r_recv), (l_send, l_recv)
-    far_right, far_left = (rr_send, rr_recv), (ll_send, ll_recv)
-
-    def halves(q):
+    hops = ((far, far_x, 2), (right, left_x, 0), (left, right_x, 1))
+
+    def stage_own(q):
         first, last = GROUPS[q]
-        return (first, (first + last) // 2), ((first + last) // 2, last)
-
-    def sent(q):
-        yield hop(x, GROUPS[q], q, right_sems, right)
-        yield hop(x, GROUPS[q], q, left_sems, left)
-        if True:
-            yield hop(x, GROUPS[q], q, far_right, far)
-        else:
-            yield hop(left_x, halves(q)[0], q, far_right, right)
-            yield hop(right_x, halves(q)[1], q, far_left, left)
-
-    def stage_own(q):
-        for m in range(*GROUPS[q]):
-            if m == 0:
-                pl.when(core == 1)(lambda: a_copy(0).wait_recv())
-                pl.when(core == 0)(lambda: own_copy.wait())
-            else:
-                a_copy(m).wait_recv()
-        hop(x, GROUPS[q], q, right_sems, right).start()
-        hop(x, GROUPS[q], q, left_sems, left).start()
-        if True:
-            hop(x, GROUPS[q], q, far_right, far).start()
-        to_partner(x, q, 0, core).start()
-
-    def stage_near(q):
-        hop(left_x, GROUPS[q], q, right_sems, right).wait_recv()
-        to_partner(left_x, q, 1, core).start()
-        hop(right_x, GROUPS[q], q, left_sems, left).wait_recv()
-        to_partner(right_x, q, 2, core).start()
-
-    def stage_far(q):
-        if True:
-            hop(far_x, GROUPS[q], q, far_right, far).wait_recv()
-        else:
-            hop(far_x, halves(q)[0], q, far_right, right).wait_recv()
-            hop(far_x, halves(q)[1], q, far_left, left).wait_recv()
-        to_partner(far_x, q, 3, core).start()
+        landed = pages_in.at[core, x, pl.ds(first, last - first)]
+        pltpu.make_async_copy(landed, landed, a_recv.at[q]).wait()
+        for device, _, way in hops:
+            hop(x, q, way, device).start()
+
+    def stage_collect(q):
+        for device, src_x, way in hops:
+            hop(src_x, q, way, device).wait_recv()
+        to_partner(q, core).start()
 
     def stage_done(q):
-        for which, src_x in enumerate((x, left_x, right_x, far_x)):
-            to_partner(src_x, q, which, 1 - core).wait_recv()
+        to_partner(q, 1 - core).wait_recv()
 
     slots = 2 * SLOTS
 
@@ -401,34 +373,35 @@
 
     resident_keys()
     steps = len(GROUPS)
-    for step in range(steps + 3):
+    half = BLOCKS // 2
+
+    def stage_attend(q):
+        stage_done(q)
+        arrived_blocks(q, q + half)
+        if q == half - 2:
+            slot_out[0:56, :] = project(slot_lat, 0, 56)
+            slot_out[64:120, :] = project(slot_lat, 64, 56)
+        if q == half - 1:
+            slot_out[56:64, :] = project(slot_lat, 56, 8)
+            slot_out[120:128, :] = project(slot_lat, 120, 8)
+
+    for step in range(steps + 2):
         if step < 8:
             resident_block(step)
+        if step == 8:
+            res_out[...] = project(lat, 0, 128)
         if step < steps:
             stage_own(step)
-        if 1 <= step < steps + 1:
-            stage_near(step - 1)
-        if 2 <= step < steps + 2:
-            stage_far(step - 2)
         if step == 0:
             meta_first()
         if step == 1:
             meta_second()
         if step == 2:
             to_rows, arrivals = slot_rows_of()
-        if step == 8:
-            res_out[...] = project(lat, 0, 128)
-        if 3 <= step:
-            stage_done(step - 3)
-            block = step - 3
-            arrived_blocks(block, block + BLOCKS // 2)
-            half = BLOCKS // 2
-            if block == half - 2:
-                slot_out[0:56, :] = project(slot_lat, 0, 56)
-                slot_out[64:120, :] = project(slot_lat, 64, 56)
-            if block == half - 1:
-                slot_out[56:64, :] = project(slot_lat, 56, 8)
-                slot_out[120:128, :] = project(slot_lat, 120, 8)
+        if 1 <= step <= steps:
+            stage_collect(step - 1)
+        if 2 <= step:
+            stage_attend(step - 2)
 
     moved = dot(to_rows, slot_out[...])
     resident_row = (iota((128, 1), 0) % 64).astype(F32) >= arrivals
@@ -440,14 +413,12 @@
     for i in range(3):
         meta_gather(i).wait_send()
     meta_partner(core).wait_send()
-    for q in range(steps):
-        for copy in sent(q):
-            copy.wait_send()
-        for which, src_x in enumerate((x, left_x, right_x, far_x)):
-            to_partner(src_x, q, which, core).wait_send()
+    all_own = pages_in.at[core, x]
+    for way in range(3):
+        pltpu.make_async_copy(all_own, all_own, h_send.at[way]).wait()
+    pltpu.make_async_copy(pages_in.at[core], pages_in.at[core], p_send).wait()
     pl.when(core == 1)(lambda: a_copy(0).wait_send())
-    for m in range(1, SLOTS):
-        a_copy(m).wait_send()
+    pltpu.make_async_copy(packed.at[1:SLOTS], packed.at[1:SLOTS], a_send.at[1]).wait()
 
 
 def shards(
@@ -491,9 +462,8 @@
             pltpu.VMEM((2, NX, SLOTS // NX, 8, 128), F32),
             pltpu.VMEM((128, 1024), BF16),
             pltpu.VMEM((128, 1024), BF16),
-            dma((12,)), dma, dma, dma((SLOTS,)), dma((SLOTS,)),
-            groups, groups, groups, groups, groups, groups, groups, groups,
-            dma((len(GROUPS), 4)), dma((len(GROUPS), 4)), dma,
+            dma((12,)), dma, dma, dma((2,)), groups,
+            dma((3,)), dma((len(GROUPS), 3)), dma, groups,
             dma((SLOTS // NX,)), dma((SLOTS // NX,)), dma((4,)), dma((4,)), dma,
         ],
         compiler_params=pltpu.CompilerParams(

time: 67.3 us -> 66 us (0.981)
  Pallas kernels: 65.2 us -> 64.2 us
    pallas_call x1, Pallas kernels: 65.2 us -> 64.2 us  [shards(): pl.pallas_call(kernel, out_shape=jax.ShapeDtypeStruct((128, 1024), BF16),...]
where the time goes in v5:
time: 66 us; the launch traced here: 65.9 us
  Pallas kernels  64.2 us (97%)
  local copies, waits for them, and re-layouts  1.67 us (3%)
    pallas_call x1, Pallas kernels, shards(): pl.pallas_call(kernel, out_shape=jax.ShapeDtypeStruct((128, 1024), BF16),...  64.2 us
    unnamed x1, local copies, waits for them, and re-layouts  1.67 us

profile of v5, /device:TPU:1, one launch (start us, length us, event | category | flops | bytes accessed | tf_op | source)
XLA Modules:
  0.0 65.9 jit_solution(457505280460474022)
XLA Ops:
  0.0 64.2 %shard_map.118 = bf16[128,1024]{1,0:T(8,128)(2,1)} custom-call(bf16[256,576]{1,0:T(8,128)(2,1)} %bitcast.15, bf16[8,4,32]{2,1,0:T(4,128)(2,1)} %bitcast.18, s32[1,32]{1,0:T(1,128)} %bitcast.20, s32[1,32]{1,0:T(1,128)} %bitcast.21, s32[1,32]{1,0:T(1,128)} %bitcast.22, bf16[1024,576]{1,0:T(8,128)(2,1)} %bitcast.12, bf16[16,4,64]{2,1,0:T(4,128)(2,1)} %bitcast.17, ...), custom_call_target="tpu_custom_call" | custom-call | tf_op jit(solution)/shard_map/pallas_call | solution.py:445
  64.2 1.7 %copy.14 = bf16[2,64,1024]{2,1,0:T(8,128)(2,1)} copy(bf16[2,64,1024]{2,1,0:T(8,128)(2,1)} %bitcast.14) | data formatting | bytes 524288

commit v6 on v5

--- a/solution.py
+++ b/solution.py
@@ -15,6 +15,7 @@
 SLOTS = NZ * NY // 2
 BLOCKS = 2 * SLOTS // 4
 GROUPS = ((0, 6), (6, 10), (10, 14), (14, 18), (18, 22), (22, 26), (26, 30), (30, 32))
+LAST = len(GROUPS) - 1
 BIG = 1e30
 MESH = pl.DeviceIdType.MESH
 softmax_scale = (0.1 * math.log(40.0) + 1.0) ** 2 / math.sqrt(192.0)
@@ -84,7 +85,7 @@
         pltpu.make_async_copy(src, dst, in_sems.at[i])
         for i, (src, dst) in enumerate(zip(sources, places))
     ]
-    for i in range(5):
+    for i in range(2):
         fetches[i].start()
     inst, head = lax.axis_index("inst"), lax.axis_index("head")
     z, y = inst // NY, inst % NY
@@ -100,9 +101,7 @@
     target_of = target
 
     barrier = pltpu.get_barrier_semaphore()
-    for device in (partner, right, left, far):
-        pl.semaphore_signal(barrier, inc=1, device_id=device, device_id_type=MESH)
-    for m in range(SLOTS):
+    for m in reversed(range(SLOTS)):
         if m == 0:
             @pl.when(core == 1)
             def _():
@@ -110,7 +109,9 @@
         else:
             pl.semaphore_signal(barrier, inc=1, device_id=target(m), device_id_type=MESH)
 
-    for i in range(5, len(fetches)):
+    for device in (partner, right, left, far):
+        pl.semaphore_signal(barrier, inc=1, device_id=device, device_id_type=MESH)
+    for i in range(2, len(fetches)):
         fetches[i].start()
 
     own = keys.at[core]
@@ -268,6 +269,14 @@
             device_id=partner, device_id_type=MESH,
         )
 
+    def part_to_partner(src_x, q):
+        span = GROUPS[q]
+        ref = pages_in.at[core, src_x, pl.ds(span[0], span[1] - span[0])]
+        return pltpu.make_async_remote_copy(
+            src_ref=ref, dst_ref=ref, send_sem=p_send, recv_sem=p_recv.at[q],
+            device_id=partner, device_id_type=MESH,
+        )
+
     hops = ((far, far_x, 2), (right, left_x, 0), (left, right_x, 1))
 
     def stage_own(q):
@@ -276,11 +285,16 @@
         pltpu.make_async_copy(landed, landed, a_recv.at[q]).wait()
         for device, _, way in hops:
             hop(x, q, way, device).start()
+        if q == LAST:
+            part_to_partner(x, q).start()
 
     def stage_collect(q):
-        for device, src_x, way in hops:
+        for device, src_x, way in reversed(hops):
             hop(src_x, q, way, device).wait_recv()
-        to_partner(q, core).start()
+            if q == LAST:
+                part_to_partner(src_x, q).start()
+        if q != LAST:
+            to_partner(q, core).start()
 
     def stage_done(q):
         to_partner(q, 1 - core).wait_recv()

time: 66 us -> 65.7 us (level)
  no operation moved by 1% of the time
where the time goes in v6:
time: 65.7 us; the launch traced here: 65.6 us
  Pallas kernels  63.9 us (97%)
  local copies, waits for them, and re-layouts  1.67 us (3%)
    pallas_call x1, Pallas kernels, shards(): pl.pallas_call(kernel, out_shape=jax.ShapeDtypeStruct((128, 1024), BF16),...  63.9 us
    unnamed x1, local copies, waits for them, and re-layouts  1.67 us

profile of v6, /device:TPU:1, one launch (start us, length us, event | category | flops | bytes accessed | tf_op | source)
XLA Modules:
  0.0 65.6 jit_solution(772155925029804644)
XLA Ops:
  0.0 63.9 %shard_map.118 = bf16[128,1024]{1,0:T(8,128)(2,1)} custom-call(bf16[256,576]{1,0:T(8,128)(2,1)} %bitcast.15, bf16[8,4,32]{2,1,0:T(4,128)(2,1)} %bitcast.18, s32[1,32]{1,0:T(1,128)} %bitcast.20, s32[1,32]{1,0:T(1,128)} %bitcast.21, s32[1,32]{1,0:T(1,128)} %bitcast.22, bf16[1024,576]{1,0:T(8,128)(2,1)} %bitcast.12, bf16[16,4,64]{2,1,0:T(4,128)(2,1)} %bitcast.17, ...), custom_call_target="tpu_custom_call" | custom-call | tf_op jit(solution)/shard_map/pallas_call | solution.py:459
  63.9 1.7 %copy.14 = bf16[2,64,1024]{2,1,0:T(8,128)(2,1)} copy(bf16[2,64,1024]{2,1,0:T(8,128)(2,1)} %bitcast.14) | data formatting | bytes 524288

commit v7 on v6

--- a/solution.py
+++ b/solution.py
@@ -402,8 +402,6 @@
     for step in range(steps + 2):
         if step < 8:
             resident_block(step)
-        if step == 8:
-            res_out[...] = project(lat, 0, 128)
         if step < steps:
             stage_own(step)
         if step == 0:
@@ -414,6 +412,8 @@
             to_rows, arrivals = slot_rows_of()
         if 1 <= step <= steps:
             stage_collect(step - 1)
+        if step == 8:
+            res_out[...] = project(lat, 0, 128)
         if 2 <= step:
             stage_attend(step - 2)
 

time: 65.7 us -> 65.7 us (level)
  no operation moved by 1% of the time
where the time goes in v7:
time: 65.7 us; the launch traced here: 65.6 us
  Pallas kernels  63.9 us (97%)
  local copies, waits for them, and re-layouts  1.67 us (3%)
    pallas_call x1, Pallas kernels, shards(): pl.pallas_call(kernel, out_shape=jax.ShapeDtypeStruct((128, 1024), BF16),...  63.9 us
    unnamed x1, local copies, waits for them, and re-layouts  1.67 us

profile of v7, /device:TPU:1, one launch (start us, length us, event | category | flops | bytes accessed | tf_op | source)
XLA Modules:
  0.0 65.6 jit_solution(9657913923106309832)
XLA Ops:
  0.0 63.9 %shard_map.118 = bf16[128,1024]{1,0:T(8,128)(2,1)} custom-call(bf16[256,576]{1,0:T(8,128)(2,1)} %bitcast.15, bf16[8,4,32]{2,1,0:T(4,128)(2,1)} %bitcast.18, s32[1,32]{1,0:T(1,128)} %bitcast.20, s32[1,32]{1,0:T(1,128)} %bitcast.21, s32[1,32]{1,0:T(1,128)} %bitcast.22, bf16[1024,576]{1,0:T(8,128)(2,1)} %bitcast.12, bf16[16,4,64]{2,1,0:T(4,128)(2,1)} %bitcast.17, ...), custom_call_target="tpu_custom_call" | custom-call | tf_op jit(solution)/shard_map/pallas_call | solution.py:459
  63.9 1.7 %copy.14 = bf16[2,64,1024]{2,1,0:T(8,128)(2,1)} copy(bf16[2,64,1024]{2,1,0:T(8,128)(2,1)} %bitcast.14) | data formatting | bytes 524288
